TPU v7x, 512 devices: a whole 4x4x16 slice. The times are simulated.
512 devices in a mesh: row: 32 (over z, core), col: 16 (over y, x).
Axes of the slice: x: 4, y: 4, z: 16, core: 2. Of those that a mesh axis runs over, the one named last changes fastest.
Arguments:
- density: float32 [384, 13, 128, 128], P('row', None, 'col'), may hold values from -1.5 to 1.5
- pattern: int32 [384, 13], P('row'), may hold values from 0 to 1, as said below
Outputs:
- purified: float32 [384, 13, 128, 128], P('row', None, 'col')
Inputs may be any that keep to these rules, and one draw needn't show every extreme that they name: `pattern`: each block row has exactly 7 ones, placed at random slots.
All inputs are finite; a program needn't handle non-finite values.
Results may differ from a plain program's by a relative error of at most 0.0003.
Values sent between devices are 32-bit elements; how exact they have to be, the bound alone decides.
No kernel may reach another device: no remote copies, remote signals or barrier semaphores. Data moves between devices by JAX's collectives and lax.ppermute only.
A program may use at most 64 MiB of HBM per device.

v0:
```python
import jax
import jax.numpy as jnp
from jax import lax
from jax.sharding import PartitionSpec as P


def with_halo(cells, sides, width):
    for axis, dim in sides:
        count = lax.axis_size(axis)
        head = lax.slice_in_dim(cells, 0, width, axis=dim)
        tail = lax.slice_in_dim(cells, cells.shape[dim] - width, cells.shape[dim], axis=dim)
        cells = jnp.concatenate(
            [
                lax.ppermute(tail, axis, [(i, (i + 1) % count) for i in range(count)]),
                cells,
                lax.ppermute(head, axis, [((i + 1) % count, i) for i in range(count)]),
            ],
            axis=dim,
        )
    return cells


def shards(density, pattern):
    block_rows, band_slots, shard_cols, block_size = density.shape
    half_band = (band_slots - 1) // 2
    span_slots = 2 * band_slots - 1
    masked = density * pattern[:, :, None, None].astype(jnp.float32)
    slot_range = jnp.arange(band_slots, dtype=jnp.int32)
    slot_list = jnp.broadcast_to(slot_range[None, :], (block_rows, band_slots))
    extended = with_halo(masked, (("row", 0),), half_band)
    row_range = jnp.arange(block_rows, dtype=jnp.int32)
    span_range = jnp.arange(span_slots, dtype=jnp.int32)
    panel_piece = lax.all_gather(masked, "col", axis=2, tiled=True)

    def square_one_row(row_index):
        left_blocks = panel_piece[row_index]
        offsets = slot_list[row_index]
        right_blocks = extended[row_index + offsets]
        products = jnp.einsum(
            "sca,sdbc->sdba", left_blocks, right_blocks, precision=lax.Precision.HIGHEST
        )
        slot_place = (
            (offsets[:, None] + slot_range[None, :])[:, :, None] == span_range[None, None, :]
        ).astype(jnp.float32)
        return jnp.einsum("sdba,sde->eba", products, slot_place, precision=lax.Precision.HIGHEST)

    square = lax.map(square_one_row, row_range)
    square_ext = with_halo(square, (("row", 0),), half_band)
    cube_panel_piece = lax.all_gather(masked, "col", axis=2, tiled=True)

    def cube_one_row(row_index):
        left_blocks = cube_panel_piece[row_index]
        offsets = slot_list[row_index]
        columns = 2 * half_band - offsets[:, None] + slot_range[None, :]
        right_blocks = square_ext[(row_index + offsets)[:, None], columns]
        return jnp.einsum(
            "sca,sibc->iba", left_blocks, right_blocks, precision=lax.Precision.HIGHEST
        )

    third_power = lax.map(cube_one_row, row_range)
    band_core = square[:, half_band : half_band + band_slots]
    return (3.0 * band_core - 2.0 * third_power) * pattern[:, :, None, None].astype(jnp.float32)


def solution(mesh):
    placed = (P("row", None, "col", None), P("row", None))
    return jax.shard_map(
        shards, mesh=mesh, in_specs=placed, out_specs=P("row", None, "col", None), check_vma=False
    )
```

profile of v0, /device:TPU:1, one launch (start us, length us, event | category | flops | bytes accessed | tf_op | source)
XLA Modules:
  0.0 314.6 jit_solution(3525062158268850795)
XLA Ops:
  7.2 2.1 broadcast_multiply_fusion
  10.6 3.0 collective-permute-start
  13.6 3.9 %collective-permute-start.1 = (f32[6,13,8,128]{3,2,1,0:T(8,128)S(1)}, f32[6,13,8,128]{3,2,1,0:T(8,128)}, u32[]{:S(2)}, u32[]{:S(2)}) collective-permute-start(f32[6,13,8,128]{3,2,1,0:T(8,128)S(1)} %get-tuple-element.142), channel_id=1, source_target_pairs={{16,0},{32,16},{48,32},{64,48},{80,64},{96,80},{112,96},{128,112},... | collective-permute-start | bytes 958472 | tf_op jit(solution)/shard_map/ppermute | solution.py:16
  18.6 1.6 collective-permute-done.1
  21.2 96.6 %all-gather.2.cloned.1.call-done = f32[12,13,128,128]{3,2,1,0:T(8,128)} async-done(((f32[12,13,8,128]{3,2,1,0:T(8,128)}), f32[12,13,128,128]{3,2,1,0:T(8,128)}) %all-gather.2.cloned.1.call-update) | async-done | bytes 10223632 | tf_op jit(solution)/shard_map/all_gather | solution.py:33
  117.8 82.9 %while.22 = (s32[]{:T(128)}, f32[12,25,8,128]{3,2,1,0:T(8,128)S(1)}, s32[12]{0:T(128)S(1)}, s32[12,13]{1,0:T(8,128)S(1)}, f32[24,13,8,128]{3,2,1,0:T(8,128)S(1)}...) while((s32[]{:T(128)}, f32[12,25,8,128]{3,2,1,0:T(8,128)S(1)}, ...), condition=%wide.region_1.2_spmd.clone, body=%wide.region_0.1_spmd.clone.sunk | while | flops 317736320 | bytes 4654931 | solution.py:47
  121.6 2.4 fusion.46
  128.5 2.4 fusion.46
  135.4 2.4 fusion.46
  142.3 2.4 fusion.46
  149.2 2.4 fusion.46
  156.1 2.4 fusion.46
  163.0 2.4 fusion.46
  170.0 2.4 fusion.46
  176.9 2.4 fusion.46
  183.8 2.4 fusion.46
  190.7 2.4 fusion.46
  197.6 2.4 fusion.46
  200.8 2.7 collective-permute-start.2
  203.5 7.1 %collective-permute-done.2 = f32[6,25,8,128]{3,2,1,0:T(8,128)S(1)} collective-permute-done((f32[6,25,8,128]{3,2,1,0:T(8,128)S(1)}, f32[6,25,8,128]{3,2,1,0:T(8,128)S(1)}, u32[]{:S(2)}, u32[]{:S(2)}) %collective-permute-start.2) | collective-permute-done | bytes 614432 | tf_op jit(solution)/shard_map/ppermute | solution.py:14
  210.6 2.6 collective-permute-done.3
  213.2 1.6 pad_maximum_fusion
  214.8 90.6 %while.23 = (s32[]{:T(128)}, f32[12,13,8,128]{3,2,1,0:T(8,128)}, s32[12]{0:T(128)S(1)}, s32[12,13]{1,0:T(8,128)S(1)}, f32[24,25,8,128]{3,2,1,0:T(8,128)S(1)}, /*...) while((s32[]{:T(128)}, f32[12,13,8,128]{3,2,1,0:T(8,128)}, s32[12]{0:T(128)S(1)}, ...), condition=%wide.region_3.4_spmd.clone, body=%wide.region_2.3_spmd.clone.sunk | while | flops 265815296 | bytes 2986247 | solution.py:60
  218.2 1.6 gather_fusion.1
  219.8 2.6 fusion.52
  225.7 1.6 gather_fusion.1
  227.3 2.6 fusion.52
  233.3 1.6 gather_fusion.1
  234.9 2.6 fusion.52
  240.8 1.6 gather_fusion.1
  242.4 2.6 fusion.52
  248.4 1.6 gather_fusion.1
  250.0 2.6 fusion.52
  255.9 1.6 gather_fusion.1
  257.5 2.6 fusion.52
  263.5 1.6 gather_fusion.1
  265.1 2.6 fusion.52
  271.0 1.6 gather_fusion.1
  272.6 2.6 fusion.52
  278.6 1.6 gather_fusion.1
  280.1 2.6 fusion.52
  286.1 1.6 gather_fusion.1
  287.7 2.6 fusion.52
  293.7 1.6 gather_fusion.1
  295.2 2.6 fusion.52
  301.2 1.6 gather_fusion.1
  302.8 2.6 fusion.52
  305.4 2.3 subtract_multiply_fusion
  (174 shorter events, 51.5 us)
Async XLA Ops:
  6.5 111.3 %all-gather.2.cloned.1.call-start = ((), (), s32[]{:S(2)}) async-start(), calls=%async_computation | async-start | bytes 10862592 | tf_op jit(solution)/shard_map/all_gather | solution.py:33
  9.4 10.8 %copy-start = (f32[12,13,8,128]{3,2,1,0:T(8,128)S(1)}, f32[12,13,8,128]{3,2,1,0:T(8,128)}, u32[]{:S(2)}) copy-start(f32[12,13,8,128]{3,2,1,0:T(8,128)} %broadcast_multiply_fusion) | copy-start | bytes 1916932
  10.6 8.0 %collective-permute-start = (f32[6,13,8,128]{3,2,1,0:T(8,128)S(1)}, f32[6,13,8,128]{3,2,1,0:T(8,128)S(1)}, u32[]{:S(2)}, u32[]{:S(2)}) collective-permute-start(f32[6,13,8,128]{3,2,1,0:T(8,128)S(1)} %get-tuple-element.141), channel_id=1, source_target_pairs={{0,16},{16,32},{32,48},{48,64},{64,80},{80,96},{96,112},{112,128},... | collective-permute-start | bytes 958472 | tf_op jit(solution)/shard_map/ppermute | solution.py:14
  13.6 6.5 %collective-permute-start.1 = (f32[6,13,8,128]{3,2,1,0:T(8,128)S(1)}, f32[6,13,8,128]{3,2,1,0:T(8,128)}, u32[]{:S(2)}, u32[]{:S(2)}) collective-permute-start(f32[6,13,8,128]{3,2,1,0:T(8,128)S(1)} %get-tuple-element.142), channel_id=1, source_target_pairs={{16,0},{32,16},{48,32},{64,48},{80,64},{96,80},{112,96},{128,112},... | collective-permute-start | bytes 958472 | tf_op jit(solution)/shard_map/ppermute | solution.py:16
  200.7 9.9 %copy-start.1 = (f32[12,25,8,128]{3,2,1,0:T(8,128)}, f32[12,25,8,128]{3,2,1,0:T(8,128)S(1)}, u32[]{:S(2)}) copy-start(f32[12,25,8,128]{3,2,1,0:T(8,128)S(1)} %get-tuple-element.84) | copy-start | bytes 3686404
  200.8 9.8 %collective-permute-start.2 = (f32[6,25,8,128]{3,2,1,0:T(8,128)S(1)}, f32[6,25,8,128]{3,2,1,0:T(8,128)S(1)}, u32[]{:S(2)}, u32[]{:S(2)}) collective-permute-start(f32[6,25,8,128]{3,2,1,0:T(8,128)S(1)} %get-tuple-element.139), channel_id=1, source_target_pairs={{0,16},{16,32},{32,48},{48,64},{64,80},{80,96},{96,112},{112,128},... | collective-permute-start | bytes 1843208 | tf_op jit(solution)/shard_map/ppermute | solution.py:14
  203.5 9.7 %collective-permute-start.3 = (f32[6,25,8,128]{3,2,1,0:T(8,128)S(1)}, f32[6,25,8,128]{3,2,1,0:T(8,128)}, u32[]{:S(2)}, u32[]{:S(2)}) collective-permute-start(f32[6,25,8,128]{3,2,1,0:T(8,128)S(1)} %get-tuple-element.140), channel_id=1, source_target_pairs={{16,0},{32,16},{48,32},{64,48},{80,64},{96,80},{112,96},{128,112},... | collective-permute-start | bytes 1843208 | tf_op jit(solution)/shard_map/ppermute | solution.py:16
Sparse Core Ops, SparseCore 0:
  10.3 107.3 all-gather.1
where the time goes:
time: 317 us; the launch traced here: 315 us
  waiting for transfers between devices  109 us (34%)
  matrix products  67.2 us (21%)
  loops' own time  47.1 us (15%)
  local copies, waits for them, and re-layouts  43.6 us (14%)
  other arithmetic  24.7 us (8%)
  between operations  13.4 us (4%)
  starting transfers between devices  9.64 us (3%)
    all_gather x1, waiting for transfers between devices, shards(): panel_piece = lax.all_gather(masked, 'col', axis=2, tiled=True)  96.6 us
    dot_general x12, matrix products, cube_one_row(): jnp.einsum('sca,sibc->iba', left_blocks, right_blocks, precision=lax.Prec...  31.6 us
    dot_general x12, matrix products, square_one_row(): jnp.einsum('sca,sdbc->sdba', left_blocks, right_blocks, precision=lax.Pre...  28.7 us
    another operation x1, loops' own time, shards(): square = lax.map(square_one_row, row_range)  24.2 us
    another operation x1, loops' own time, shards(): third_power = lax.map(cube_one_row, row_range)  22.9 us
    gather x12, local copies, waits for them, and re-layouts, cube_one_row(): right_blocks = square_ext[(row_index + offsets)[:, None], columns]  18.7 us
    dynamic_slice x24, local copies, waits for them, and re-layouts, shards(): square = lax.map(square_one_row, row_range)  14.6 us
    concatenate x24, other arithmetic, cube_one_row(): right_blocks = square_ext[(row_index + offsets)[:, None], columns]  8.61 us
  transfers between devices with their start and end apart: 5, of which 5 were waited for; matrix products, arithmetic and copies ran while one was open for 1% of the time, Pallas kernels for 0%

commit v1 on v0

v1 whole, which is shorter than its diff:
```python
import functools

import jax
import jax.numpy as jnp
from jax import lax
from jax.experimental import pallas as pl
from jax.experimental.pallas import tpu as pltpu
from jax.sharding import PartitionSpec as P

HALF = 6
SLOTS = 13
ONES = 7
COLS = 8
B = 128
CHUNK = HALF * ONES
PAIRS = HALF // 2
VIEW = 14 * COLS
WIDE = 26 * COLS
HALO = 18 * COLS
DEPTH = 14 * B
NEAR = (-1, 1, 2)
F32 = jnp.float32
BF16 = jnp.bfloat16
AXES = ("row", "col")


def flipped(core, index, last):
    return jnp.where(core == 0, index, last - index)


def split(value):
    high = value.astype(BF16)
    return high, (value - high.astype(F32)).astype(BF16)


def prepare(pattern, density, packed, dense0, dense1, slots):
    core = lax.rem(lax.axis_index("row"), 2)
    for chunk, dense in enumerate((dense0, dense1)):

        @pl.loop(0, HALF)
        def _(v):
            u = chunk * HALF + v
            r = flipped(core, u, 2 * HALF - 1)
            rank = jnp.int32(0)
            for s in range(SLOTS):
                place = flipped(core, s, SLOTS - 1)
                on = pattern[r, place]
                dense[v, s] = density[r, place] * on.astype(F32)
                slots[rank] = place
                rank = rank + on
            for t in range(ONES):
                packed[u * ONES + t] = density[r, slots[t]]


def paired(first, second):
    gap = jnp.zeros((COLS, B), F32)
    return jnp.concatenate(
        [jnp.concatenate([first, gap], axis=0), jnp.concatenate([gap, second], axis=0)], axis=1
    )


def square_kernel(chunk, pattern, own, a1m, a1p, a1o, a2m, a2p, a2o, far_m, far_p, far_o, before, middle, after,
                  square, halo, w_high_out, w_low_out, raw, w_high, w_low, sides, slots, raw_sems, out_sems):
    core = lax.rem(lax.axis_index("row"), 2)
    col = lax.axis_index("col")
    y, x = col // 4, lax.rem(col, 4)

    def place(step1, step2):
        down = jnp.where(core == 0, step2, step1)
        over = jnp.where(core == 0, step1, step2)
        return pl.multiple_of(((y + down + 4) % 4 * 4 + (x + over + 4) % 4) * COLS, COLS)

    first = chunk * CHUNK
    sources = [(own.at[pl.ds(first, CHUNK)], 0, 0)]
    for ref, step in zip((a1m, a1p, a1o), NEAR):
        sources.append((ref.at[pl.ds(first, CHUNK)], step, 0))
    for ref, step in zip((a2m, a2p, a2o), NEAR):
        sources.append((ref.at[pl.ds(first, CHUNK)], 0, step))
    for ref, step in zip((far_m, far_p, far_o), NEAR):
        for i, other in enumerate(NEAR):
            sources.append((ref.at[pl.ds(i * CHUNK, CHUNK)], other, step))
    copies = []
    for i, (ref, step1, step2) in enumerate(sources):
        copies.append(
            pltpu.make_async_copy(ref, raw.at[:, pl.ds(place(step1, step2), COLS), :], raw_sems.at[i])
        )
        copies[-1].start()

    def other_way(ref, v):
        return jnp.concatenate([ref[HALF - 1 - v, SLOTS - 1 - s] for s in range(SLOTS)], axis=0)

    def same_way(ref, v):
        return jnp.concatenate([ref[v, s] for s in range(SLOTS)], axis=0)

    for part, ref in enumerate((before, middle, after)):
        turned = part == (0 if chunk == 0 else 2)
        take = other_way if turned else same_way
        for i in range(PAIRS):
            high, low = split(paired(take(ref, 2 * i), take(ref, 2 * i + 1)))
            sides[part * PAIRS + i, :VIEW] = high
            sides[part * PAIRS + i, VIEW:] = low

    for i in range(PAIRS):
        w_high[i] = jnp.zeros((DEPTH, 2 * B), BF16)
        w_low[i] = jnp.zeros((DEPTH, 2 * B), BF16)
    for v in range(HALF):
        r = flipped(core, chunk * HALF + v, 2 * HALF - 1)
        rank = jnp.int32(0)
        for s in range(SLOTS):
            slots[v * 8 + rank] = s
            rank = rank + pattern[r, flipped(core, s, SLOTS - 1)]
    for copy in copies:
        copy.wait()
    outs = []
    for i in range(PAIRS):
        for q in range(2):
            v = 2 * i + q
            for t in range(ONES):
                high, low = split(raw[v * ONES + t])
                rows = pl.ds(pl.multiple_of((slots[v * 8 + t] + q) * B, B), B)
                w_high[i, rows, q * B : (q + 1) * B] = high
                w_low[i, rows, q * B : (q + 1) * B] = low
        for k, (here, there) in enumerate(((w_high, w_high_out), (w_low, w_low_out))):
            outs.append(pltpu.make_async_copy(here.at[i], there.at[i], out_sems.at[2 * i + k]))
            outs[-1].start()

    for i in range(PAIRS):
        square[i] = jnp.zeros((WIDE, 2 * B), F32)
        for m in range(7):
            depth = slice(m * 2 * B, (m + 1) * 2 * B)
            whole = jnp.dot(sides[i + m], w_high[i, depth], preferred_element_type=F32)
            small = jnp.dot(sides[i + m, :VIEW], w_low[i, depth], preferred_element_type=F32)
            square[i, 2 * COLS * m : 2 * COLS * m + VIEW] += whole[:VIEW] + whole[VIEW:] + small
        if chunk == 0:
            halo[i] = square[i, :HALO]
        else:
            halo[i] = square[i, WIDE - HALO :]
    for copy in outs:
        copy.wait()


def lift(ref, held):
    for i in range(PAIRS):
        held[0, i], held[1, i] = split(ref[i])


def lift_halo(ref, held, first):
    for i in range(PAIRS):
        source = ref[PAIRS - 1 - i]
        turned = jnp.concatenate(
            [source[(HALO // COLS - 1 - j) * COLS : (HALO // COLS - j) * COLS] for j in range(HALO // COLS)], axis=0
        )
        turned = jnp.concatenate([turned[:, B:], turned[:, :B]], axis=1)
        held[0, i, first : first + HALO], held[1, i, first : first + HALO] = split(turned)


def add_products(total, held, part, w_high, w_low):
    for i in range(PAIRS):
        value = None
        for k in range(PAIRS):
            m = part * PAIRS + k - i
            if m < 0 or m > 6:
                continue
            rows = slice(2 * COLS * (6 - m), 2 * COLS * (6 - m) + VIEW)
            depth = slice(m * 2 * B, (m + 1) * 2 * B)
            high, low = held[0, k, rows], held[1, k, rows]
            term = (
                jnp.dot(high, w_high[i, depth], preferred_element_type=F32)
                + jnp.dot(low, w_high[i, depth], preferred_element_type=F32)
                + jnp.dot(high, w_low[i, depth], preferred_element_type=F32)
            )
            value = term if value is None else value + term
        total[i] += value


def third_first(halo, square0, w_high, w_low, total, held_halo, held):
    total[...] = jnp.zeros_like(total)
    lift(square0, held)
    lift_halo(halo, held_halo, WIDE - HALO)
    add_products(total, held, 1, w_high, w_low)
    add_products(total, held_halo, 0, w_high, w_low)


def third_second(square0, square1, w_high0, w_low0, w_high1, w_low1, before, total0, total1, held0, held1):
    lift(square0, held0)
    lift(square1, held1)
    total0[...] = before[...]
    total1[...] = jnp.zeros_like(total1)
    add_products(total0, held1, 2, w_high0, w_low0)
    add_products(total1, held0, 0, w_high1, w_low1)
    add_products(total1, held1, 1, w_high1, w_low1)


def finish(pattern, halo, square0, square1, w_high1, w_low1, total0, before1, out, total1, held):
    core = lax.rem(lax.axis_index("row"), 2)
    lift_halo(halo, held, 0)
    total1[...] = before1[...]
    add_products(total1, held, 2, w_high1, w_low1)
    for chunk, (square, total) in enumerate(((square0, total0), (square1, total1))):
        for i in range(PAIRS):
            value = 3.0 * square[i, 6 * COLS : 6 * COLS + VIEW] - 2.0 * total[i]
            for q in range(2):
                r = flipped(core, chunk * HALF + 2 * i + q, 2 * HALF - 1)
                for s in range(SLOTS):
                    place = flipped(core, s, SLOTS - 1)
                    tile = value[(s + q) * COLS : (s + q + 1) * COLS, q * B : (q + 1) * B]
                    out[r, place] = tile * pattern[r, place].astype(F32)


ANY = pl.BlockSpec(memory_space=pl.ANY)
VMEM = pl.BlockSpec(memory_space=pltpu.VMEM)
SMEM = pl.BlockSpec(memory_space=pltpu.SMEM)
PARAMS = pltpu.CompilerParams(vmem_limit_bytes=48 * 1024 * 1024)


def cost(products):
    flops = 2 * products * 3 * VIEW * 256 * 256
    return pl.CostEstimate(flops=flops, bytes_accessed=4_000_000, transcendentals=0)


def shape(*dims, dtype=F32):
    return jax.ShapeDtypeStruct(dims, dtype)


def shards(density, pattern):
    spots = [(z, c, y, x) for z in range(16) for c in range(2) for y in range(4) for x in range(4)]

    def number(z, c, y, x):
        return (z % 16 * 2 + c) * 16 + y % 4 * 4 + x % 4

    def send(value, move):
        return lax.ppermute(value, AXES, [(number(*spot), number(*move(*spot))) for spot in spots])

    def first_way(step):
        return lambda z, c, y, x: (z, c, y, x + step) if c == 0 else (z, c, y + step, x)

    def second_way(step):
        return lambda z, c, y, x: (z, c, y + step, x) if c == 0 else (z, c, y, x + step)

    def next_chip(z, c, y, x):
        return (z - 1, 1, y, x) if c == 0 else (z + 1, 0, y, x)

    def other_core(z, c, y, x):
        return (z, 1 - c, y, x)

    packed, dense0, dense1 = pl.pallas_call(
        prepare,
        out_shape=(shape(2 * CHUNK, COLS, B), shape(HALF, SLOTS, COLS, B), shape(HALF, SLOTS, COLS, B)),
        in_specs=[SMEM, VMEM],
        out_specs=(VMEM, VMEM, VMEM),
        scratch_shapes=[pltpu.SMEM((8,), jnp.int32)],
        compiler_params=PARAMS,
        name="prepare",
    )(pattern, density)

    steps = (1, -1, 2)
    along1 = [send(packed, first_way(step)) for step in steps]
    along2 = [send(packed, second_way(step)) for step in steps]
    halo_z = send(dense0, next_chip)
    halo_c = send(dense1, other_core)
    far = []
    for chunk in range(2):
        three = jnp.concatenate([piece[chunk * CHUNK : (chunk + 1) * CHUNK] for piece in along1])
        far.append([send(three, second_way(step)) for step in steps])

    weights = shape(PAIRS, DEPTH, 2 * B, dtype=BF16)

    def squared(chunk, before, middle, after):
        return pl.pallas_call(
            functools.partial(square_kernel, chunk),
            out_shape=(shape(PAIRS, WIDE, 2 * B), shape(PAIRS, HALO, 2 * B), weights, weights),
            in_specs=[SMEM] + [ANY] * 10 + [VMEM] * 3,
            out_specs=(VMEM, VMEM, ANY, ANY),
            scratch_shapes=[
                pltpu.VMEM((CHUNK, B, B), F32),
                pltpu.VMEM((PAIRS, DEPTH, 2 * B), BF16),
                pltpu.VMEM((PAIRS, DEPTH, 2 * B), BF16),
                pltpu.VMEM((3 * PAIRS, 2 * VIEW, 2 * B), BF16),
                pltpu.SMEM((HALF * 8,), jnp.int32),
                pltpu.SemaphoreType.DMA((16,)),
                pltpu.SemaphoreType.DMA((2 * PAIRS,)),
            ],
            compiler_params=PARAMS,
            cost_estimate=cost(21),
            name=f"square{chunk}",
        )(pattern, packed, *along1, *along2, *far[chunk], before, middle, after)

    square0, edge0, w_high0, w_low0 = squared(0, halo_z, dense0, dense1)
    square_z = send(edge0, next_chip)
    totals = shape(PAIRS, VIEW, 2 * B)
    held = pltpu.VMEM((2, PAIRS, WIDE, 2 * B), BF16)
    total0 = pl.pallas_call(
        third_first,
        out_shape=totals,
        in_specs=[VMEM] * 4,
        out_specs=VMEM,
        scratch_shapes=[held, held],
        compiler_params=PARAMS,
        cost_estimate=cost(15),
        name="third_first",
    )(square_z, square0, w_high0, w_low0)
    square1, edge1, w_high1, w_low1 = squared(1, dense0, dense1, halo_c)
    square_c = send(edge1, other_core)
    total0, total1 = pl.pallas_call(
        third_second,
        out_shape=(totals, totals),
        in_specs=[VMEM] * 7,
        out_specs=(VMEM, VMEM),
        scratch_shapes=[held, held],
        compiler_params=PARAMS,
        cost_estimate=cost(21),
        name="third_second",
    )(square0, square1, w_high0, w_low0, w_high1, w_low1, total0)
    return pl.pallas_call(
        finish,
        out_shape=shape(2 * HALF, SLOTS, COLS, B),
        in_specs=[SMEM] + [VMEM] * 7,
        out_specs=VMEM,
        scratch_shapes=[pltpu.VMEM((PAIRS, VIEW, 2 * B), F32), held],
        compiler_params=PARAMS,
        cost_estimate=cost(6),
        name="finish",
    )(pattern, square_c, square0, square1, w_high1, w_low1, total0, total1)


def solution(mesh):
    placed = (P("row", None, "col", None), P("row", None))
    return jax.shard_map(
        shards, mesh=mesh, in_specs=placed, out_specs=P("row", None, "col", None), check_vma=False
    )
```

time: 317 us -> 90.3 us (0.28)
  waiting for transfers between devices: 109 us -> 1.77 us
  matrix products: 67.2 us -> 0 us
  starting transfers between devices: 9.64 us -> 64.7 us
  loops' own time: 47.1 us -> 0 us
  local copies, waits for them, and re-layouts: 43.6 us -> 1.86 us
  other arithmetic: 24.7 us -> 0.07 us
  Pallas kernels: 0 us -> 20.9 us
  between operations: 13.4 us -> 0.35 us
    all_gather x1 -> x0, waiting for transfers between devices: 96.6 us -> none  [shards(): panel_piece = lax.all_gather(masked, 'col', axis=2, tiled=True)]
    dot_general x36 -> x0, matrix products: 67.2 us -> none  [the longest x12 31.6 us: cube_one_row(): jnp.einsum('sca,sibc->iba', left_blocks, right_blocks, precision=lax.Prec...]
    ppermute x4 -> x16, starting transfers between devices: 9.64 us -> 64.7 us  [send(): lax.ppermute(value, AXES, [(number(*spot), number(*move(*spot))) for spot...]
    another operation x2 -> x0, loops' own time: 47.1 us -> none  [the longest x1 24.2 us: shards(): square = lax.map(square_one_row, row_range)]
    gather x24 -> x0, local copies, waits for them, and re-layouts: 25.8 us -> none  [the longest x12 18.7 us: cube_one_row(): right_blocks = square_ext[(row_index + offsets)[:, None], columns]]
    pallas_call x0 -> x6, Pallas kernels: none -> 20.9 us  [the longest x2 8.47 us: squared(): pl.pallas_call(functools.partial(square_kernel, chunk), out_shape=(shape(...]
    dynamic_slice x24 -> x0, local copies, waits for them, and re-layouts: 14.6 us -> none  [shards(): square = lax.map(square_one_row, row_range)]
    concatenate x26 -> x2, other arithmetic: 11.3 us -> 0.07 us  [shards(): jnp.concatenate([piece[chunk * CHUNK:(chunk + 1) * CHUNK] for piece in al...]
  transfers between devices with their start and end apart: 5 -> 16, of which waited for: 5 -> 1; matrix products, arithmetic and copies ran while one was open for 1% -> 0% of each run, Pallas kernels for 0% -> 18%
where the time goes in v1:
time: 90.3 us; the launch traced here: 89.6 us
  starting transfers between devices  64.7 us (72%)
  Pallas kernels  20.9 us (23%)
  local copies, waits for them, and re-layouts  1.86 us (2%)
  waiting for transfers between devices  1.77 us (2%)
    ppermute x16, starting transfers between devices, send(): lax.ppermute(value, AXES, [(number(*spot), number(*move(*spot))) for spot...  64.7 us
    pallas_call x2, Pallas kernels, squared(): pl.pallas_call(functools.partial(square_kernel, chunk), out_shape=(shape(...  8.47 us
    pallas_call x1, Pallas kernels, shards(): pl.pallas_call(third_second, out_shape=(totals, totals), in_specs=[VMEM]...  4.93 us
    pallas_call x1, Pallas kernels, shards(): pl.pallas_call(finish, out_shape=shape(2 * HALF, SLOTS, COLS, B), in_spec...  3.25 us
    pallas_call x1, Pallas kernels, shards(): pl.pallas_call(third_first, out_shape=totals, in_specs=[VMEM] * 4, out_sp...  2.81 us
  transfers between devices with their start and end apart: 16, of which 1 were waited for; matrix products, arithmetic and copies ran while one was open for 0% of the time, Pallas kernels for 18%

profile of v1, /device:TPU:1, one launch (start us, length us, event | category | flops | bytes accessed | tf_op | source)
XLA Modules:
  0.0 89.6 jit_solution(1490470252867859430)
XLA Ops:
  0.0 0.0 copy-start.2
  0.0 1.1 %copy-done.2 = f32[12,13,8,128]{3,2,1,0:T(8,128)S(1)} copy-done((f32[12,13,8,128]{3,2,1,0:T(8,128)S(1)}, f32[12,13,8,128]{3,2,1,0:T(8,128)}, u32[]{:S(2)}) %copy-start.2) | copy-done | bytes 639000
  1.1 0.0 copy-start.3
  1.1 0.7 copy-done.3
  1.8 1.4 %prepare.1 = (f32[84,8,128]{2,1,0:T(8,128)S(1)}, f32[6,13,8,128]{3,2,1,0:T(8,128)S(1)}, f32[6,13,8,128]{3,2,1,0:T(8,128)S(1)}) custom-call(s32[12,13]{1,0:T(8,128)S(1)} %copy-done.3, f32[12,13,8,128]{3,2,1,0:T(8,128)S(1)} %copy-done.2), custom_call_target="tpu_custom_call" | custom-call | tf_op jit(solution)/shard_map/prepare/pallas_call | solution.py:246
  3.2 5.7 %collective-permute-start.2 = (f32[84,8,128]{2,1,0:T(8,128)S(1)}, f32[84,8,128]{2,1,0:T(8,128)S(1)}, u32[]{:S(2)}, u32[]{:S(2)}) collective-permute-start(f32[84,8,128]{2,1,0:T(8,128)S(1)} %get-tuple-element.18.own), channel_id=1, source_target_pairs={{0,2},{1,3},{2,0},{3,1},{4,6},{5,7},{6,4},{7,5},{8,10},{9,11},{10,... | collective-permute-start | bytes 1032200 | tf_op jit(solution)/shard_map/ppermute | solution.py:232
  8.9 2.7 %collective-permute-start.1 = (f32[84,8,128]{2,1,0:T(8,128)S(1)}, f32[84,8,128]{2,1,0:T(8,128)S(1)}, u32[]{:S(2)}, u32[]{:S(2)}) collective-permute-start(f32[84,8,128]{2,1,0:T(8,128)S(1)} %get-tuple-element.18.own), channel_id=1, source_target_pairs={{0,3},{1,0},{2,1},{3,2},{4,7},{5,4},{6,5},{7,6},{8,11},{9,8},{10,9... | collective-permute-start | bytes 1032200 | tf_op jit(solution)/shard_map/ppermute | solution.py:232
  11.6 2.6 %collective-permute-start = (f32[84,8,128]{2,1,0:T(8,128)S(1)}, f32[84,8,128]{2,1,0:T(8,128)S(1)}, u32[]{:S(2)}, u32[]{:S(2)}) collective-permute-start(f32[84,8,128]{2,1,0:T(8,128)S(1)} %get-tuple-element.18.own), channel_id=1, source_target_pairs={{0,1},{1,2},{2,3},{3,0},{4,5},{5,6},{6,7},{7,4},{8,9},{9,10},{10,1... | collective-permute-start | bytes 1032200 | tf_op jit(solution)/shard_map/ppermute | solution.py:232
  14.2 4.8 %collective-permute-start.14 = (f32[6,13,8,128]{3,2,1,0:T(8,128)S(1)}, f32[6,13,8,128]{3,2,1,0:T(8,128)S(1)}, u32[]{:S(2)}, u32[]{:S(2)}) collective-permute-start(f32[6,13,8,128]{3,2,1,0:T(8,128)S(1)} %get-tuple-element.19.before.middle), channel_id=1, source_target_pairs={{0,496},{1,497},{2,498},{3,499},{4,500},{5,501},{6,502},{7,503},{8... | collective-permute-start | bytes 958472 | tf_op jit(solution)/shard_map/ppermute | solution.py:232
  19.0 0.0 collective-permute-done.2.a1o
  19.0 0.0 collective-permute-done.1.a1p
  19.1 1.7 %collective-permute-done.a1m = f32[84,8,128]{2,1,0:T(8,128)S(1)} collective-permute-done((f32[84,8,128]{2,1,0:T(8,128)S(1)}, f32[84,8,128]{2,1,0:T(8,128)S(1)}, u32[]{:S(2)}, u32[]{:S(2)}) %collective-permute-start) | collective-permute-done | bytes 344096 | tf_op jit(solution)/shard_map/ppermute | solution.py:232
  20.9 4.7 %collective-permute-start.13 = (f32[126,8,128]{2,1,0:T(8,128)S(1)}, f32[126,8,128]{2,1,0:T(8,128)S(1)}, u32[]{:S(2)}, u32[]{:S(2)}) collective-permute-start(f32[126,8,128]{2,1,0:T(8,128)S(1)} %pad_maximum_fusion.1), channel_id=1, source_target_pairs={{0,8},{1,9},{2,10},{3,11},{4,12},{5,13},{6,14},{7,15},{8,0},{9,1},... | collective-permute-start | bytes 1548296 | tf_op jit(solution)/shard_map/ppermute | solution.py:232
  25.5 2.1 %collective-permute-start.5 = (f32[84,8,128]{2,1,0:T(8,128)S(1)}, f32[84,8,128]{2,1,0:T(8,128)S(1)}, u32[]{:S(2)}, u32[]{:S(2)}) collective-permute-start(f32[84,8,128]{2,1,0:T(8,128)S(1)} %get-tuple-element.18.own), channel_id=1, source_target_pairs={{0,8},{1,9},{2,10},{3,11},{4,12},{5,13},{6,14},{7,15},{8,0},{9,1},... | collective-permute-start | bytes 1032200 | tf_op jit(solution)/shard_map/ppermute | solution.py:232
  27.7 4.4 %collective-permute-start.4 = (f32[84,8,128]{2,1,0:T(8,128)S(1)}, f32[84,8,128]{2,1,0:T(8,128)S(1)}, u32[]{:S(2)}, u32[]{:S(2)}) collective-permute-start(f32[84,8,128]{2,1,0:T(8,128)S(1)} %get-tuple-element.18.own), channel_id=1, source_target_pairs={{0,12},{1,13},{2,14},{3,15},{4,0},{5,1},{6,2},{7,3},{8,4},{9,5},{1... | collective-permute-start | bytes 1032200 | tf_op jit(solution)/shard_map/ppermute | solution.py:232
  32.0 1.9 %collective-permute-start.3 = (f32[84,8,128]{2,1,0:T(8,128)S(1)}, f32[84,8,128]{2,1,0:T(8,128)S(1)}, u32[]{:S(2)}, u32[]{:S(2)}) collective-permute-start(f32[84,8,128]{2,1,0:T(8,128)S(1)} %get-tuple-element.18.own), channel_id=1, source_target_pairs={{0,4},{1,5},{2,6},{3,7},{4,8},{5,9},{6,10},{7,11},{8,12},{9,13},{1... | collective-permute-start | bytes 1032200 | tf_op jit(solution)/shard_map/ppermute | solution.py:232
  34.0 0.0 collective-permute-done.14.before
  34.0 4.6 %collective-permute-start.12 = (f32[126,8,128]{2,1,0:T(8,128)S(1)}, f32[126,8,128]{2,1,0:T(8,128)S(1)}, u32[]{:S(2)}, u32[]{:S(2)}) collective-permute-start(f32[126,8,128]{2,1,0:T(8,128)S(1)} %pad_maximum_fusion.1), channel_id=1, source_target_pairs={{0,12},{1,13},{2,14},{3,15},{4,0},{5,1},{6,2},{7,3},{8,4},{9,5},{1... | collective-permute-start | bytes 1548296 | tf_op jit(solution)/shard_map/ppermute | solution.py:232
  38.6 0.0 collective-permute-done.5.a2o
  38.6 1.9 %collective-permute-start.11 = (f32[126,8,128]{2,1,0:T(8,128)S(1)}, f32[126,8,128]{2,1,0:T(8,128)S(1)}, u32[]{:S(2)}, u32[]{:S(2)}) collective-permute-start(f32[126,8,128]{2,1,0:T(8,128)S(1)} %pad_maximum_fusion.1), channel_id=1, source_target_pairs={{0,4},{1,5},{2,6},{3,7},{4,8},{5,9},{6,10},{7,11},{8,12},{9,13},{1... | collective-permute-start | bytes 1548296 | tf_op jit(solution)/shard_map/ppermute | solution.py:232
  40.5 0.0 collective-permute-done.4.a2p
  40.6 3.2 %collective-permute-start.8 = (f32[126,8,128]{2,1,0:T(8,128)S(1)}, f32[126,8,128]{2,1,0:T(8,128)S(1)}, u32[]{:S(2)}, u32[]{:S(2)}) collective-permute-start(f32[126,8,128]{2,1,0:T(8,128)S(1)} %pad_maximum_fusion), channel_id=1, source_target_pairs={{0,8},{1,9},{2,10},{3,11},{4,12},{5,13},{6,14},{7,15},{8,0},{9,1},... | collective-permute-start | bytes 1548296 | tf_op jit(solution)/shard_map/ppermute | solution.py:232
  43.8 0.0 collective-permute-done.3.a2m
  43.8 3.5 %collective-permute-start.7 = (f32[126,8,128]{2,1,0:T(8,128)S(1)}, f32[126,8,128]{2,1,0:T(8,128)S(1)}, u32[]{:S(2)}, u32[]{:S(2)}) collective-permute-start(f32[126,8,128]{2,1,0:T(8,128)S(1)} %pad_maximum_fusion), channel_id=1, source_target_pairs={{0,12},{1,13},{2,14},{3,15},{4,0},{5,1},{6,2},{7,3},{8,4},{9,5},{1... | collective-permute-start | bytes 1548296 | tf_op jit(solution)/shard_map/ppermute | solution.py:232
  47.3 0.0 collective-permute-done.13.far_o
  47.3 2.3 %collective-permute-start.6 = (f32[126,8,128]{2,1,0:T(8,128)S(1)}, f32[126,8,128]{2,1,0:T(8,128)S(1)}, u32[]{:S(2)}, u32[]{:S(2)}) collective-permute-start(f32[126,8,128]{2,1,0:T(8,128)S(1)} %pad_maximum_fusion), channel_id=1, source_target_pairs={{0,4},{1,5},{2,6},{3,7},{4,8},{5,9},{6,10},{7,11},{8,12},{9,13},{1... | collective-permute-start | bytes 1548296 | tf_op jit(solution)/shard_map/ppermute | solution.py:232
  49.6 0.0 collective-permute-done.12.far_p
  49.6 8.7 %collective-permute-start.9 = (f32[6,13,8,128]{3,2,1,0:T(8,128)S(1)}, f32[6,13,8,128]{3,2,1,0:T(8,128)S(1)}, u32[]{:S(2)}, u32[]{:S(2)}) collective-permute-start(f32[6,13,8,128]{3,2,1,0:T(8,128)S(1)} %get-tuple-element.20.middle.after), channel_id=1, source_target_pairs={{0,16},{1,17},{2,18},{3,19},{4,20},{5,21},{6,22},{7,23},{8,24},{9,... | collective-permute-start | bytes 958472 | tf_op jit(solution)/shard_map/ppermute | solution.py:232
  58.3 0.0 collective-permute-done.11.far_m
  58.3 4.3 %square0.1 = (f32[3,208,256]{2,1,0:T(8,128)S(1)}, f32[3,144,256]{2,1,0:T(8,128)S(1)}, bf16[3,1792,256]{2,1,0:T(8,128)(2,1)}, bf16[3,1792,256]{2,1,0:T(8,128)(2,1)}) custom-call(s32[12,13]{1,0:T(8,128)S(1)} %copy-done.3, f32[84,8,128]{2,1,0:T(8,128)S(1)} %get-tuple-element.18.own, f32[84,8,128]{2,1,0:T(8,128)S(1)} %collective-permute-done.a1m, ...), custom_call_target="tpu_custom_call" | custom-call | flops 924844032 | bytes 4000000 | tf_op jit(solution)/shard_map/square0/pallas_call | solution.py:269
  62.6 0.0 copy-start.1
  62.6 5.6 %collective-permute-start.15 = (f32[3,144,256]{2,1,0:T(8,128)S(1)}, f32[3,144,256]{2,1,0:T(8,128)S(1)}, u32[]{:S(2)}, u32[]{:S(2)}) collective-permute-start(f32[3,144,256]{2,1,0:T(8,128)S(1)} %get-tuple-element.28), channel_id=1, source_target_pairs={{0,496},{1,497},{2,498},{3,499},{4,500},{5,501},{6,502},{7,503},{8... | collective-permute-start | bytes 1327112 | tf_op jit(solution)/shard_map/ppermute | solution.py:232
  68.2 0.0 collective-permute-done.9.after
  68.2 0.0 collective-permute-done.8.far_o
  68.2 0.0 collective-permute-done.7.far_p
  68.2 0.0 collective-permute-done.6.far_m
  68.2 4.2 %square1.1 = (f32[3,208,256]{2,1,0:T(8,128)S(1)}, f32[3,144,256]{2,1,0:T(8,128)S(1)}, bf16[3,1792,256]{2,1,0:T(8,128)(2,1)}, bf16[3,1792,256]{2,1,0:T(8,128)(2,1)}) custom-call(s32[12,13]{1,0:T(8,128)S(1)} %copy-done.3, f32[84,8,128]{2,1,0:T(8,128)S(1)} %get-tuple-element.18.own, f32[84,8,128]{2,1,0:T(8,128)S(1)} %collective-permute-done.a1m, ...), custom_call_target="tpu_custom_call" | custom-call | flops 924844032 | bytes 4000000 | tf_op jit(solution)/shard_map/square1/pallas_call | solution.py:269
  72.5 6.1 %collective-permute-start.10 = (f32[3,144,256]{2,1,0:T(8,128)S(1)}, f32[3,144,256]{2,1,0:T(8,128)S(1)}, u32[]{:S(2)}, u32[]{:S(2)}) collective-permute-start(f32[3,144,256]{2,1,0:T(8,128)S(1)} %get-tuple-element.21), channel_id=1, source_target_pairs={{0,16},{1,17},{2,18},{3,19},{4,20},{5,21},{6,22},{7,23},{8,24},{9,... | collective-permute-start | bytes 1327112 | tf_op jit(solution)/shard_map/ppermute | solution.py:232
  78.5 0.0 collective-permute-done.15.halo
  78.6 0.0 copy-done.1
  78.6 2.8 %third_first.1.before = f32[3,112,256]{2,1,0:T(8,128)S(1)} custom-call(f32[3,144,256]{2,1,0:T(8,128)S(1)} %collective-permute-done.15.halo, f32[3,208,256]{2,1,0:T(8,128)S(1)} %get-tuple-element.22.square0, bf16[3,1792,256]{2,1,0:T(8,128)(2,1)S(1)} %copy-done.1, bf16[3,1792,256]{2,1,0:T(8,128)(2,1)} %get-tuple-element.27.w_low.w_low0), custom_call_target="tpu_custom_call" | custom-call | flops 660602880 | bytes 4000000 | tf_op jit(solution)/shard_map/third_first/pallas_call | solution.py:292
  81.4 0.0 copy-start
  81.4 4.9 %third_second.1 = (f32[3,112,256]{2,1,0:T(8,128)S(1)}, f32[3,112,256]{2,1,0:T(8,128)S(1)}) custom-call(f32[3,208,256]{2,1,0:T(8,128)S(1)} %get-tuple-element.22.square0, f32[3,208,256]{2,1,0:T(8,128)S(1)} %get-tuple-element.23.square1, bf16[3,1792,256]{2,1,0:T(8,128)(2,1)S(1)} %copy-done.1, bf16[3,1792,256]{2,1,0:T(8,128)(2,1)} %get-tuple-element.27.w_low.w_low0, ...), custom_call_target="tpu_custom_call" | custom-call | flops 924844032 | bytes 4000000 | tf_op jit(solution)/shard_map/third_second/pallas_call | solution.py:304
  86.3 0.0 collective-permute-done.10.halo
  86.3 0.0 copy-done
  86.4 3.3 %finish.1 = f32[12,13,8,128]{3,2,1,0:T(8,128)} custom-call(s32[12,13]{1,0:T(8,128)S(1)} %copy-done.3, f32[3,144,256]{2,1,0:T(8,128)S(1)} %collective-permute-done.10.halo, f32[3,208,256]{2,1,0:T(8,128)S(1)} %get-tuple-element.22.square0, f32[3,208,256]{2,1,0:T(8,128)S(1)} %get-tuple-element.23.square1, bf16[3,1792,256]{2,1,0:T(8,128)(2,1)S(1)} %copy-done, ...), custom_call_target="tpu_custom_call" | custom-call | flops 264241152 | bytes 4000000 | tf_op jit(solution)/shard_map/finish/pallas_call | solution.py:314
  (5 shorter events, 0.1 us)
Async XLA Ops:
  0.0 1.1 %copy-start.2 = (f32[12,13,8,128]{3,2,1,0:T(8,128)S(1)}, f32[12,13,8,128]{3,2,1,0:T(8,128)}, u32[]{:S(2)}) copy-start(f32[12,13,8,128]{3,2,1,0:T(8,128)} %density.1) | copy-start | bytes 1916932
  1.1 0.7 copy-start.3
  3.2 15.7 %collective-permute-start.2 = (f32[84,8,128]{2,1,0:T(8,128)S(1)}, f32[84,8,128]{2,1,0:T(8,128)S(1)}, u32[]{:S(2)}, u32[]{:S(2)}) collective-permute-start(f32[84,8,128]{2,1,0:T(8,128)S(1)} %get-tuple-element.18.own), channel_id=1, source_target_pairs={{0,2},{1,3},{2,0},{3,1},{4,6},{5,7},{6,4},{7,5},{8,10},{9,11},{10,... | collective-permute-start | bytes 1032200 | tf_op jit(solution)/shard_map/ppermute | solution.py:232
  8.9 10.1 %collective-permute-start.1 = (f32[84,8,128]{2,1,0:T(8,128)S(1)}, f32[84,8,128]{2,1,0:T(8,128)S(1)}, u32[]{:S(2)}, u32[]{:S(2)}) collective-permute-start(f32[84,8,128]{2,1,0:T(8,128)S(1)} %get-tuple-element.18.own), channel_id=1, source_target_pairs={{0,3},{1,0},{2,1},{3,2},{4,7},{5,4},{6,5},{7,6},{8,11},{9,8},{10,9... | collective-permute-start | bytes 1032200 | tf_op jit(solution)/shard_map/ppermute | solution.py:232
  11.6 9.2 %collective-permute-start = (f32[84,8,128]{2,1,0:T(8,128)S(1)}, f32[84,8,128]{2,1,0:T(8,128)S(1)}, u32[]{:S(2)}, u32[]{:S(2)}) collective-permute-start(f32[84,8,128]{2,1,0:T(8,128)S(1)} %get-tuple-element.18.own), channel_id=1, source_target_pairs={{0,1},{1,2},{2,3},{3,0},{4,5},{5,6},{6,7},{7,4},{8,9},{9,10},{10,1... | collective-permute-start | bytes 1032200 | tf_op jit(solution)/shard_map/ppermute | solution.py:232
  14.2 19.8 %collective-permute-start.14 = (f32[6,13,8,128]{3,2,1,0:T(8,128)S(1)}, f32[6,13,8,128]{3,2,1,0:T(8,128)S(1)}, u32[]{:S(2)}, u32[]{:S(2)}) collective-permute-start(f32[6,13,8,128]{3,2,1,0:T(8,128)S(1)} %get-tuple-element.19.before.middle), channel_id=1, source_target_pairs={{0,496},{1,497},{2,498},{3,499},{4,500},{5,501},{6,502},{7,503},{8... | collective-permute-start | bytes 958472 | tf_op jit(solution)/shard_map/ppermute | solution.py:232
  20.9 26.4 %collective-permute-start.13 = (f32[126,8,128]{2,1,0:T(8,128)S(1)}, f32[126,8,128]{2,1,0:T(8,128)S(1)}, u32[]{:S(2)}, u32[]{:S(2)}) collective-permute-start(f32[126,8,128]{2,1,0:T(8,128)S(1)} %pad_maximum_fusion.1), channel_id=1, source_target_pairs={{0,8},{1,9},{2,10},{3,11},{4,12},{5,13},{6,14},{7,15},{8,0},{9,1},... | collective-permute-start | bytes 1548296 | tf_op jit(solution)/shard_map/ppermute | solution.py:232
  25.5 13.1 %collective-permute-start.5 = (f32[84,8,128]{2,1,0:T(8,128)S(1)}, f32[84,8,128]{2,1,0:T(8,128)S(1)}, u32[]{:S(2)}, u32[]{:S(2)}) collective-permute-start(f32[84,8,128]{2,1,0:T(8,128)S(1)} %get-tuple-element.18.own), channel_id=1, source_target_pairs={{0,8},{1,9},{2,10},{3,11},{4,12},{5,13},{6,14},{7,15},{8,0},{9,1},... | collective-permute-start | bytes 1032200 | tf_op jit(solution)/shard_map/ppermute | solution.py:232
  27.7 12.9 %collective-permute-start.4 = (f32[84,8,128]{2,1,0:T(8,128)S(1)}, f32[84,8,128]{2,1,0:T(8,128)S(1)}, u32[]{:S(2)}, u32[]{:S(2)}) collective-permute-start(f32[84,8,128]{2,1,0:T(8,128)S(1)} %get-tuple-element.18.own), channel_id=1, source_target_pairs={{0,12},{1,13},{2,14},{3,15},{4,0},{5,1},{6,2},{7,3},{8,4},{9,5},{1... | collective-permute-start | bytes 1032200 | tf_op jit(solution)/shard_map/ppermute | solution.py:232
  32.0 11.7 %collective-permute-start.3 = (f32[84,8,128]{2,1,0:T(8,128)S(1)}, f32[84,8,128]{2,1,0:T(8,128)S(1)}, u32[]{:S(2)}, u32[]{:S(2)}) collective-permute-start(f32[84,8,128]{2,1,0:T(8,128)S(1)} %get-tuple-element.18.own), channel_id=1, source_target_pairs={{0,4},{1,5},{2,6},{3,7},{4,8},{5,9},{6,10},{7,11},{8,12},{9,13},{1... | collective-permute-start | bytes 1032200 | tf_op jit(solution)/shard_map/ppermute | solution.py:232
  34.0 15.6 %collective-permute-start.12 = (f32[126,8,128]{2,1,0:T(8,128)S(1)}, f32[126,8,128]{2,1,0:T(8,128)S(1)}, u32[]{:S(2)}, u32[]{:S(2)}) collective-permute-start(f32[126,8,128]{2,1,0:T(8,128)S(1)} %pad_maximum_fusion.1), channel_id=1, source_target_pairs={{0,12},{1,13},{2,14},{3,15},{4,0},{5,1},{6,2},{7,3},{8,4},{9,5},{1... | collective-permute-start | bytes 1548296 | tf_op jit(solution)/shard_map/ppermute | solution.py:232
  38.6 19.7 %collective-permute-start.11 = (f32[126,8,128]{2,1,0:T(8,128)S(1)}, f32[126,8,128]{2,1,0:T(8,128)S(1)}, u32[]{:S(2)}, u32[]{:S(2)}) collective-permute-start(f32[126,8,128]{2,1,0:T(8,128)S(1)} %pad_maximum_fusion.1), channel_id=1, source_target_pairs={{0,4},{1,5},{2,6},{3,7},{4,8},{5,9},{6,10},{7,11},{8,12},{9,13},{1... | collective-permute-start | bytes 1548296 | tf_op jit(solution)/shard_map/ppermute | solution.py:232
  40.6 27.7 %collective-permute-start.8 = (f32[126,8,128]{2,1,0:T(8,128)S(1)}, f32[126,8,128]{2,1,0:T(8,128)S(1)}, u32[]{:S(2)}, u32[]{:S(2)}) collective-permute-start(f32[126,8,128]{2,1,0:T(8,128)S(1)} %pad_maximum_fusion), channel_id=1, source_target_pairs={{0,8},{1,9},{2,10},{3,11},{4,12},{5,13},{6,14},{7,15},{8,0},{9,1},... | collective-permute-start | bytes 1548296 | tf_op jit(solution)/shard_map/ppermute | solution.py:232
  43.8 24.5 %collective-permute-start.7 = (f32[126,8,128]{2,1,0:T(8,128)S(1)}, f32[126,8,128]{2,1,0:T(8,128)S(1)}, u32[]{:S(2)}, u32[]{:S(2)}) collective-permute-start(f32[126,8,128]{2,1,0:T(8,128)S(1)} %pad_maximum_fusion), channel_id=1, source_target_pairs={{0,12},{1,13},{2,14},{3,15},{4,0},{5,1},{6,2},{7,3},{8,4},{9,5},{1... | collective-permute-start | bytes 1548296 | tf_op jit(solution)/shard_map/ppermute | solution.py:232
  47.3 20.9 %collective-permute-start.6 = (f32[126,8,128]{2,1,0:T(8,128)S(1)}, f32[126,8,128]{2,1,0:T(8,128)S(1)}, u32[]{:S(2)}, u32[]{:S(2)}) collective-permute-start(f32[126,8,128]{2,1,0:T(8,128)S(1)} %pad_maximum_fusion), channel_id=1, source_target_pairs={{0,4},{1,5},{2,6},{3,7},{4,8},{5,9},{6,10},{7,11},{8,12},{9,13},{1... | collective-permute-start | bytes 1548296 | tf_op jit(solution)/shard_map/ppermute | solution.py:232
  49.6 18.6 %collective-permute-start.9 = (f32[6,13,8,128]{3,2,1,0:T(8,128)S(1)}, f32[6,13,8,128]{3,2,1,0:T(8,128)S(1)}, u32[]{:S(2)}, u32[]{:S(2)}) collective-permute-start(f32[6,13,8,128]{3,2,1,0:T(8,128)S(1)} %get-tuple-element.20.middle.after), channel_id=1, source_target_pairs={{0,16},{1,17},{2,18},{3,19},{4,20},{5,21},{6,22},{7,23},{8,24},{9,... | collective-permute-start | bytes 958472 | tf_op jit(solution)/shard_map/ppermute | solution.py:232
  62.6 16.0 %copy-start.1 = (bf16[3,1792,256]{2,1,0:T(8,128)(2,1)S(1)}, bf16[3,1792,256]{2,1,0:T(8,128)(2,1)}, u32[]{:S(2)}) copy-start(bf16[3,1792,256]{2,1,0:T(8,128)(2,1)} %get-tuple-element.26.w_high.w_high0) | copy-start | bytes 8257540
  62.6 16.0 %collective-permute-start.15 = (f32[3,144,256]{2,1,0:T(8,128)S(1)}, f32[3,144,256]{2,1,0:T(8,128)S(1)}, u32[]{:S(2)}, u32[]{:S(2)}) collective-permute-start(f32[3,144,256]{2,1,0:T(8,128)S(1)} %get-tuple-element.28), channel_id=1, source_target_pairs={{0,496},{1,497},{2,498},{3,499},{4,500},{5,501},{6,502},{7,503},{8... | collective-permute-start | bytes 1327112 | tf_op jit(solution)/shard_map/ppermute | solution.py:232
  72.5 13.9 %collective-permute-start.10 = (f32[3,144,256]{2,1,0:T(8,128)S(1)}, f32[3,144,256]{2,1,0:T(8,128)S(1)}, u32[]{:S(2)}, u32[]{:S(2)}) collective-permute-start(f32[3,144,256]{2,1,0:T(8,128)S(1)} %get-tuple-element.21), channel_id=1, source_target_pairs={{0,16},{1,17},{2,18},{3,19},{4,20},{5,21},{6,22},{7,23},{8,24},{9,... | collective-permute-start | bytes 1327112 | tf_op jit(solution)/shard_map/ppermute | solution.py:232
  81.4 5.0 %copy-start = (bf16[3,1792,256]{2,1,0:T(8,128)(2,1)S(1)}, bf16[3,1792,256]{2,1,0:T(8,128)(2,1)}, u32[]{:S(2)}) copy-start(bf16[3,1792,256]{2,1,0:T(8,128)(2,1)} %get-tuple-element.24.w_high1) | copy-start | bytes 8257540

commit v2 on v1

--- a/solution.py
+++ b/solution.py
@@ -18,7 +18,6 @@
 WIDE = 26 * COLS
 HALO = 18 * COLS
 DEPTH = 14 * B
-NEAR = (-1, 1, 2)
 F32 = jnp.float32
 BF16 = jnp.bfloat16
 AXES = ("row", "col")
@@ -49,7 +48,9 @@
                 slots[rank] = place
                 rank = rank + on
             for t in range(ONES):
-                packed[u * ONES + t] = density[r, slots[t]]
+                tile = density[r, slots[t]]
+                for copy in range(4):
+                    packed[copy, u * ONES + t] = tile
 
 
 def paired(first, second):
@@ -59,32 +60,20 @@
     )
 
 
-def square_kernel(chunk, pattern, own, a1m, a1p, a1o, a2m, a2p, a2o, far_m, far_p, far_o, before, middle, after,
-                  square, halo, w_high_out, w_low_out, raw, w_high, w_low, sides, slots, raw_sems, out_sems):
+def square_kernel(chunk, pattern, near, far_m, far_p, far_o, before, middle, after,
+                  square, halo, w_high, w_low, raw, sides, slots):
     core = lax.rem(lax.axis_index("row"), 2)
     col = lax.axis_index("col")
     y, x = col // 4, lax.rem(col, 4)
 
-    def place(step1, step2):
-        down = jnp.where(core == 0, step2, step1)
-        over = jnp.where(core == 0, step1, step2)
-        return pl.multiple_of(((y + down + 4) % 4 * 4 + (x + over + 4) % 4) * COLS, COLS)
-
-    first = chunk * CHUNK
-    sources = [(own.at[pl.ds(first, CHUNK)], 0, 0)]
-    for ref, step in zip((a1m, a1p, a1o), NEAR):
-        sources.append((ref.at[pl.ds(first, CHUNK)], step, 0))
-    for ref, step in zip((a2m, a2p, a2o), NEAR):
-        sources.append((ref.at[pl.ds(first, CHUNK)], 0, step))
-    for ref, step in zip((far_m, far_p, far_o), NEAR):
-        for i, other in enumerate(NEAR):
-            sources.append((ref.at[pl.ds(i * CHUNK, CHUNK)], other, step))
-    copies = []
-    for i, (ref, step1, step2) in enumerate(sources):
-        copies.append(
-            pltpu.make_async_copy(ref, raw.at[:, pl.ds(place(step1, step2), COLS), :], raw_sems.at[i])
-        )
-        copies[-1].start()
+    second = jnp.where(core == 0, y, x)
+    for ref, base, step in ((near, chunk * CHUNK, 0), (far_m, 0, -1), (far_p, 0, 1), (far_o, 0, 2)):
+        other = lax.rem(second + step + 4, 4)
+        for i in range(4):
+            spot = jnp.where(core == 0, other * 4 + i, i * 4 + other)
+            rows = pl.ds(pl.multiple_of(spot * COLS, COLS), COLS)
+            for t in range(CHUNK):
+                raw[t, rows, :] = ref[i, base + t]
 
     def other_way(ref, v):
         return jnp.concatenate([ref[HALF - 1 - v, SLOTS - 1 - s] for s in range(SLOTS)], axis=0)
@@ -109,9 +98,6 @@
         for s in range(SLOTS):
             slots[v * 8 + rank] = s
             rank = rank + pattern[r, flipped(core, s, SLOTS - 1)]
-    for copy in copies:
-        copy.wait()
-    outs = []
     for i in range(PAIRS):
         for q in range(2):
             v = 2 * i + q
@@ -120,9 +106,6 @@
                 rows = pl.ds(pl.multiple_of((slots[v * 8 + t] + q) * B, B), B)
                 w_high[i, rows, q * B : (q + 1) * B] = high
                 w_low[i, rows, q * B : (q + 1) * B] = low
-        for k, (here, there) in enumerate(((w_high, w_high_out), (w_low, w_low_out))):
-            outs.append(pltpu.make_async_copy(here.at[i], there.at[i], out_sems.at[2 * i + k]))
-            outs[-1].start()
 
     for i in range(PAIRS):
         square[i] = jnp.zeros((WIDE, 2 * B), F32)
@@ -135,8 +118,6 @@
             halo[i] = square[i, :HALO]
         else:
             halo[i] = square[i, WIDE - HALO :]
-    for copy in outs:
-        copy.wait()
 
 
 def lift(ref, held):
@@ -207,10 +188,9 @@
                     out[r, place] = tile * pattern[r, place].astype(F32)
 
 
-ANY = pl.BlockSpec(memory_space=pl.ANY)
 VMEM = pl.BlockSpec(memory_space=pltpu.VMEM)
 SMEM = pl.BlockSpec(memory_space=pltpu.SMEM)
-PARAMS = pltpu.CompilerParams(vmem_limit_bytes=48 * 1024 * 1024)
+PARAMS = pltpu.CompilerParams(vmem_limit_bytes=16 * 1024 * 1024)
 
 
 def cost(products):
@@ -231,9 +211,6 @@
     def send(value, move):
         return lax.ppermute(value, AXES, [(number(*spot), number(*move(*spot))) for spot in spots])
 
-    def first_way(step):
-        return lambda z, c, y, x: (z, c, y, x + step) if c == 0 else (z, c, y + step, x)
-
     def second_way(step):
         return lambda z, c, y, x: (z, c, y + step, x) if c == 0 else (z, c, y, x + step)
 
@@ -245,7 +222,7 @@
 
     packed, dense0, dense1 = pl.pallas_call(
         prepare,
-        out_shape=(shape(2 * CHUNK, COLS, B), shape(HALF, SLOTS, COLS, B), shape(HALF, SLOTS, COLS, B)),
+        out_shape=(shape(4, 2 * CHUNK, COLS, B), shape(HALF, SLOTS, COLS, B), shape(HALF, SLOTS, COLS, B)),
         in_specs=[SMEM, VMEM],
         out_specs=(VMEM, VMEM, VMEM),
         scratch_shapes=[pltpu.SMEM((8,), jnp.int32)],
@@ -253,15 +230,18 @@
         name="prepare",
     )(pattern, density)
 
-    steps = (1, -1, 2)
-    along1 = [send(packed, first_way(step)) for step in steps]
-    along2 = [send(packed, second_way(step)) for step in steps]
+    quads = []
+    for z in range(16):
+        for i in range(4):
+            quads.append([number(z, 0, i, x) for x in range(4)])
+            quads.append([number(z, 1, y, i) for y in range(4)])
+    near = lax.all_to_all(packed, AXES, 0, 0, axis_index_groups=quads)
+    far = []
+    for chunk in range(2):
+        part = near[:, chunk * CHUNK : (chunk + 1) * CHUNK]
+        far.append([send(part, second_way(step)) for step in (1, -1, 2)])
     halo_z = send(dense0, next_chip)
     halo_c = send(dense1, other_core)
-    far = []
-    for chunk in range(2):
-        three = jnp.concatenate([piece[chunk * CHUNK : (chunk + 1) * CHUNK] for piece in along1])
-        far.append([send(three, second_way(step)) for step in steps])
 
     weights = shape(PAIRS, DEPTH, 2 * B, dtype=BF16)
 
@@ -269,21 +249,17 @@
         return pl.pallas_call(
             functools.partial(square_kernel, chunk),
             out_shape=(shape(PAIRS, WIDE, 2 * B), shape(PAIRS, HALO, 2 * B), weights, weights),
-            in_specs=[SMEM] + [ANY] * 10 + [VMEM] * 3,
-            out_specs=(VMEM, VMEM, ANY, ANY),
+            in_specs=[SMEM] + [VMEM] * 7,
+            out_specs=(VMEM, VMEM, VMEM, VMEM),
             scratch_shapes=[
                 pltpu.VMEM((CHUNK, B, B), F32),
-                pltpu.VMEM((PAIRS, DEPTH, 2 * B), BF16),
-                pltpu.VMEM((PAIRS, DEPTH, 2 * B), BF16),
                 pltpu.VMEM((3 * PAIRS, 2 * VIEW, 2 * B), BF16),
                 pltpu.SMEM((HALF * 8,), jnp.int32),
-                pltpu.SemaphoreType.DMA((16,)),
-                pltpu.SemaphoreType.DMA((2 * PAIRS,)),
             ],
             compiler_params=PARAMS,
             cost_estimate=cost(21),
             name=f"square{chunk}",
-        )(pattern, packed, *along1, *along2, *far[chunk], before, middle, after)
+        )(pattern, near, *far[chunk], before, middle, after)
 
     square0, edge0, w_high0, w_low0 = squared(0, halo_z, dense0, dense1)
     square_z = send(edge0, next_chip)
@@ -299,6 +275,7 @@
         cost_estimate=cost(15),
         name="third_first",
     )(square_z, square0, w_high0, w_low0)
+    total0, halo_c = lax.optimization_barrier((total0, halo_c))
     square1, edge1, w_high1, w_low1 = squared(1, dense0, dense1, halo_c)
     square_c = send(edge1, other_core)
     total0, total1 = pl.pallas_call(

time: 90.3 us -> 76.3 us (0.84)
  starting transfers between devices: 64.7 us -> 40.7 us
  blocking collectives: 0 us -> 16.3 us
  Pallas kernels: 20.9 us -> 12.4 us
  waiting for transfers between devices: 1.77 us -> 4.33 us
    ppermute x16 -> x10, starting transfers between devices: 64.7 us -> 40.7 us  [send(): lax.ppermute(value, AXES, [(number(*spot), number(*move(*spot))) for spot...]
    all_to_all x0 -> x1, blocking collectives: none -> 16.3 us  [shards(): near = lax.all_to_all(packed, AXES, 0, 0, axis_index_groups=quads)]
    pallas_call x1, Pallas kernels: 4.93 us -> 1.35 us  [shards(): pl.pallas_call(third_second, out_shape=(totals, totals), in_specs=[VMEM]...]
    ppermute x16 -> x10, waiting for transfers between devices: 1.77 us -> 4.33 us  [send(): lax.ppermute(value, AXES, [(number(*spot), number(*move(*spot))) for spot...]
    pallas_call x2, Pallas kernels: 8.47 us -> 6.49 us  [squared(): pl.pallas_call(functools.partial(square_kernel, chunk), out_shape=(shape(...]
    pallas_call x1, Pallas kernels: 2.81 us -> 1 us  [shards(): pl.pallas_call(third_first, out_shape=totals, in_specs=[VMEM] * 4, out_sp...]
    pallas_call x1, Pallas kernels: 3.25 us -> 2.14 us  [shards(): pl.pallas_call(finish, out_shape=shape(2 * HALF, SLOTS, COLS, B), in_spec...]
  transfers between devices with their start and end apart: 16 -> 10, of which waited for: 1 -> 2; matrix products, arithmetic and copies ran while one was open for 0% -> 0% of each run, Pallas kernels for 18% -> 7%
where the time goes in v2:
time: 76.3 us; the launch traced here: 75.8 us
  starting transfers between devices  40.7 us (53%)
  blocking collectives  16.3 us (21%)
  Pallas kernels  12.4 us (16%)
  waiting for transfers between devices  4.33 us (6%)
  local copies, waits for them, and re-layouts  1.87 us (2%)
    ppermute x10, starting transfers between devices, send(): lax.ppermute(value, AXES, [(number(*spot), number(*move(*spot))) for spot...  40.7 us
    all_to_all x1, blocking collectives, shards(): near = lax.all_to_all(packed, AXES, 0, 0, axis_index_groups=quads)  16.3 us
    pallas_call x2, Pallas kernels, squared(): pl.pallas_call(functools.partial(square_kernel, chunk), out_shape=(shape(...  6.49 us
    ppermute x10, waiting for transfers between devices, send(): lax.ppermute(value, AXES, [(number(*spot), number(*move(*spot))) for spot...  4.33 us
    pallas_call x1, Pallas kernels, shards(): pl.pallas_call(finish, out_shape=shape(2 * HALF, SLOTS, COLS, B), in_spec...  2.14 us
    unnamed x6, local copies, waits for them, and re-layouts  1.78 us
  transfers between devices with their start and end apart: 10, of which 2 were waited for; matrix products, arithmetic and copies ran while one was open for 0% of the time, Pallas kernels for 7%

profile of v2, /device:TPU:1, one launch (start us, length us, event | category | flops | bytes accessed | tf_op | source)
XLA Modules:
  0.0 75.8 jit_solution(16715295271856508333)
XLA Ops:
  0.0 0.0 copy-start
  0.0 1.1 %copy-done = f32[12,13,8,128]{3,2,1,0:T(8,128)S(1)} copy-done((f32[12,13,8,128]{3,2,1,0:T(8,128)S(1)}, f32[12,13,8,128]{3,2,1,0:T(8,128)}, u32[]{:S(2)}) %copy-start) | copy-done | bytes 639000
  1.1 0.0 copy-start.1
  1.1 0.7 copy-done.1
  1.8 1.4 %prepare.1 = (f32[4,84,8,128]{3,2,1,0:T(8,128)S(1)}, f32[6,13,8,128]{3,2,1,0:T(8,128)S(1)}, f32[6,13,8,128]{3,2,1,0:T(8,128)S(1)}) custom-call(s32[12,13]{1,0:T(8,128)S(1)} %copy-done.1, f32[12,13,8,128]{3,2,1,0:T(8,128)S(1)} %copy-done), custom_call_target="tpu_custom_call" | custom-call | tf_op jit(solution)/shard_map/prepare/pallas_call | solution.py:223
  3.2 16.3 %all_to_all.5.near = f32[4,84,8,128]{3,2,1,0:T(8,128)S(1)} all-to-all(f32[4,84,8,128]{3,2,1,0:T(8,128)S(1)} %get-tuple-element.20), channel_id=1, replica_groups={{0,1,2,3},{16,20,24,28},{4,5,6,7},{17,21,25,29},{8,9,10,11},{18,22,26,3..., dimensions={0} | all-to-all | bytes 2752512 | tf_op jit(solution)/shard_map/all_to_all | solution.py:238
  19.5 0.1 fusion
  19.6 4.7 %collective-permute-start.5 = (f32[4,42,8,128]{3,2,1,0:T(8,128)S(1)}, f32[4,42,8,128]{3,2,1,0:T(8,128)S(1)}, u32[]{:S(2)}, u32[]{:S(2)}) collective-permute-start(f32[4,42,8,128]{3,2,1,0:T(8,128)S(1)} %get-tuple-element.35), channel_id=1, source_target_pairs={{0,8},{1,9},{2,10},{3,11},{4,12},{5,13},{6,14},{7,15},{8,0},{9,1},... | collective-permute-start | bytes 2064392 | tf_op jit(solution)/shard_map/ppermute | solution.py:212
  24.3 2.8 %collective-permute-start.4 = (f32[4,42,8,128]{3,2,1,0:T(8,128)S(1)}, f32[4,42,8,128]{3,2,1,0:T(8,128)S(1)}, u32[]{:S(2)}, u32[]{:S(2)}) collective-permute-start(f32[4,42,8,128]{3,2,1,0:T(8,128)S(1)} %get-tuple-element.35), channel_id=1, source_target_pairs={{0,12},{1,13},{2,14},{3,15},{4,0},{5,1},{6,2},{7,3},{8,4},{9,5},{1... | collective-permute-start | bytes 2064392 | tf_op jit(solution)/shard_map/ppermute | solution.py:212
  27.1 2.5 %collective-permute-start.3 = (f32[4,42,8,128]{3,2,1,0:T(8,128)S(1)}, f32[4,42,8,128]{3,2,1,0:T(8,128)S(1)}, u32[]{:S(2)}, u32[]{:S(2)}) collective-permute-start(f32[4,42,8,128]{3,2,1,0:T(8,128)S(1)} %get-tuple-element.35), channel_id=1, source_target_pairs={{0,4},{1,5},{2,6},{3,7},{4,8},{5,9},{6,10},{7,11},{8,12},{9,13},{1... | collective-permute-start | bytes 2064392 | tf_op jit(solution)/shard_map/ppermute | solution.py:212
  29.6 6.4 %collective-permute-start.6 = (f32[6,13,8,128]{3,2,1,0:T(8,128)S(1)}, f32[6,13,8,128]{3,2,1,0:T(8,128)S(1)}, u32[]{:S(2)}, u32[]{:S(2)}) collective-permute-start(f32[6,13,8,128]{3,2,1,0:T(8,128)S(1)} %get-tuple-element.21.middle.before), channel_id=1, source_target_pairs={{0,496},{1,497},{2,498},{3,499},{4,500},{5,501},{6,502},{7,503},{8... | collective-permute-start | bytes 958472 | tf_op jit(solution)/shard_map/ppermute | solution.py:212
  36.0 2.6 %collective-permute-start.2 = (f32[4,42,8,128]{3,2,1,0:T(8,128)S(1)}, f32[4,42,8,128]{3,2,1,0:T(8,128)S(1)}, u32[]{:S(2)}, u32[]{:S(2)}) collective-permute-start(f32[4,42,8,128]{3,2,1,0:T(8,128)S(1)} %get-tuple-element.36), channel_id=1, source_target_pairs={{0,8},{1,9},{2,10},{3,11},{4,12},{5,13},{6,14},{7,15},{8,0},{9,1},... | collective-permute-start | bytes 2064392 | tf_op jit(solution)/shard_map/ppermute | solution.py:212
  38.6 2.3 %collective-permute-done.6.before = f32[6,13,8,128]{3,2,1,0:T(8,128)S(1)} collective-permute-done((f32[6,13,8,128]{3,2,1,0:T(8,128)S(1)}, f32[6,13,8,128]{3,2,1,0:T(8,128)S(1)}, u32[]{:S(2)}, u32[]{:S(2)}) %collective-permute-start.6) | collective-permute-done | bytes 319520 | tf_op jit(solution)/shard_map/ppermute | solution.py:212
  40.9 2.8 %collective-permute-start.1 = (f32[4,42,8,128]{3,2,1,0:T(8,128)S(1)}, f32[4,42,8,128]{3,2,1,0:T(8,128)S(1)}, u32[]{:S(2)}, u32[]{:S(2)}) collective-permute-start(f32[4,42,8,128]{3,2,1,0:T(8,128)S(1)} %get-tuple-element.36), channel_id=1, source_target_pairs={{0,12},{1,13},{2,14},{3,15},{4,0},{5,1},{6,2},{7,3},{8,4},{9,5},{1... | collective-permute-start | bytes 2064392 | tf_op jit(solution)/shard_map/ppermute | solution.py:212
  43.7 0.0 collective-permute-done.5.far_o
  43.7 2.5 %collective-permute-start = (f32[4,42,8,128]{3,2,1,0:T(8,128)S(1)}, f32[4,42,8,128]{3,2,1,0:T(8,128)S(1)}, u32[]{:S(2)}, u32[]{:S(2)}) collective-permute-start(f32[4,42,8,128]{3,2,1,0:T(8,128)S(1)} %get-tuple-element.36), channel_id=1, source_target_pairs={{0,4},{1,5},{2,6},{3,7},{4,8},{5,9},{6,10},{7,11},{8,12},{9,13},{1... | collective-permute-start | bytes 2064392 | tf_op jit(solution)/shard_map/ppermute | solution.py:212
  46.2 0.0 collective-permute-done.4.far_p
  46.2 0.0 collective-permute-done.3.far_m
  46.2 3.2 %square0.1 = (f32[3,208,256]{2,1,0:T(8,128)S(1)}, f32[3,144,256]{2,1,0:T(8,128)S(1)}, bf16[3,1792,256]{2,1,0:T(8,128)(2,1)S(1)}, bf16[3,1792,256]{2,1,0:T(8,128)(2,1)S(1)}) custom-call(s32[12,13]{1,0:T(8,128)S(1)} %copy-done.1, f32[4,84,8,128]{3,2,1,0:T(8,128)S(1)} %all_to_all.5.near, f32[4,42,8,128]{3,2,1,0:T(8,128)S(1)} %collective-permute-done.3.far_m, ...), custom_call_target="tpu_custom_call" | custom-call | flops 924844032 | bytes 4000000 | tf_op jit(solution)/shard_map/square0/pallas_call | solution.py:249
  49.5 8.2 %collective-permute-start.7 = (f32[3,144,256]{2,1,0:T(8,128)S(1)}, f32[3,144,256]{2,1,0:T(8,128)S(1)}, u32[]{:S(2)}, u32[]{:S(2)}) collective-permute-start(f32[3,144,256]{2,1,0:T(8,128)S(1)} %get-tuple-element.23), channel_id=1, source_target_pairs={{0,496},{1,497},{2,498},{3,499},{4,500},{5,501},{6,502},{7,503},{8... | collective-permute-start | bytes 1327112 | tf_op jit(solution)/shard_map/ppermute | solution.py:212
  57.7 4.3 %collective-permute-start.8 = (f32[6,13,8,128]{3,2,1,0:T(8,128)S(1)}, f32[6,13,8,128]{3,2,1,0:T(8,128)S(1)}, u32[]{:S(2)}, u32[]{:S(2)}) collective-permute-start(f32[6,13,8,128]{3,2,1,0:T(8,128)S(1)} %get-tuple-element.22.after.middle), channel_id=1, source_target_pairs={{0,16},{1,17},{2,18},{3,19},{4,20},{5,21},{6,22},{7,23},{8,24},{9,... | collective-permute-start | bytes 958472 | tf_op jit(solution)/shard_map/ppermute | solution.py:212
  62.0 2.0 %collective-permute-done.7.halo = f32[3,144,256]{2,1,0:T(8,128)S(1)} collective-permute-done((f32[3,144,256]{2,1,0:T(8,128)S(1)}, f32[3,144,256]{2,1,0:T(8,128)S(1)}, u32[]{:S(2)}, u32[]{:S(2)}) %collective-permute-start.7) | collective-permute-done | bytes 442400 | tf_op jit(solution)/shard_map/ppermute | solution.py:212
  64.0 0.0 copy-start.2
  64.0 1.0 %third_first.1.before = f32[3,112,256]{2,1,0:T(8,128)S(1)} custom-call(f32[3,144,256]{2,1,0:T(8,128)S(1)} %collective-permute-done.7.halo, f32[3,208,256]{2,1,0:T(8,128)S(1)} %get-tuple-element.24.square0, bf16[3,1792,256]{2,1,0:T(8,128)(2,1)S(1)} %get-tuple-element.25.w_high.w_high0, bf16[3,1792,256]{2,1,0:T(8,128)(2,1)S(1)} %get-tuple-element.26.w_low.w_low0), custom_call_target="tpu_custom_call" | custom-call | flops 660602880 | bytes 4000000 | tf_op jit(solution)/shard_map/third_first/pallas_call | solution.py:268
  65.0 0.0 collective-permute-done.8.after
  65.0 0.0 collective-permute-done.2.far_o
  65.0 0.0 collective-permute-done.1.far_p
  65.0 0.0 collective-permute-done.far_m
  65.0 0.0 copy-done.2
  65.0 3.3 %square1.1 = (f32[3,208,256]{2,1,0:T(8,128)S(1)}, f32[3,144,256]{2,1,0:T(8,128)S(1)}, bf16[3,1792,256]{2,1,0:T(8,128)(2,1)S(1)}, bf16[3,1792,256]{2,1,0:T(8,128)(2,1)S(1)}) custom-call(s32[12,13]{1,0:T(8,128)S(1)} %copy-done.2, f32[4,84,8,128]{3,2,1,0:T(8,128)S(1)} %all_to_all.5.near, f32[4,42,8,128]{3,2,1,0:T(8,128)S(1)} %collective-permute-done.far_m, ...), custom_call_target="tpu_custom_call" | custom-call | flops 924844032 | bytes 4000000 | tf_op jit(solution)/shard_map/square1/pallas_call | solution.py:249
  68.3 4.0 %collective-permute-start.9 = (f32[3,144,256]{2,1,0:T(8,128)S(1)}, f32[3,144,256]{2,1,0:T(8,128)S(1)}, u32[]{:S(2)}, u32[]{:S(2)}) collective-permute-start(f32[3,144,256]{2,1,0:T(8,128)S(1)} %get-tuple-element.28), channel_id=1, source_target_pairs={{0,16},{1,17},{2,18},{3,19},{4,20},{5,21},{6,22},{7,23},{8,24},{9,... | collective-permute-start | bytes 1327112 | tf_op jit(solution)/shard_map/ppermute | solution.py:212
  72.3 1.3 %third_second.1 = (f32[3,112,256]{2,1,0:T(8,128)S(1)}, f32[3,112,256]{2,1,0:T(8,128)S(1)}) custom-call(f32[3,208,256]{2,1,0:T(8,128)S(1)} %get-tuple-element.24.square0, f32[3,208,256]{2,1,0:T(8,128)S(1)} %get-tuple-element.29.square1, bf16[3,1792,256]{2,1,0:T(8,128)(2,1)S(1)} %get-tuple-element.25.w_high.w_high0, ...), custom_call_target="tpu_custom_call" | custom-call | flops 924844032 | bytes 4000000 | tf_op jit(solution)/shard_map/third_second/pallas_call | solution.py:281
  73.6 0.0 collective-permute-done.9.halo
  73.7 2.1 %finish.1 = f32[12,13,8,128]{3,2,1,0:T(8,128)} custom-call(s32[12,13]{1,0:T(8,128)S(1)} %copy-done.2, f32[3,144,256]{2,1,0:T(8,128)S(1)} %collective-permute-done.9.halo, f32[3,208,256]{2,1,0:T(8,128)S(1)} %get-tuple-element.24.square0, f32[3,208,256]{2,1,0:T(8,128)S(1)} %get-tuple-element.29.square1, bf16[3,1792,256]{2,1,0:T(8,128)(2,1)S(1)} %get-tuple-element.30.w_high1, ...), custom_call_target="tpu_custom_call" | custom-call | flops 264241152 | bytes 4000000 | tf_op jit(solution)/shard_map/finish/pallas_call | solution.py:291
Async XLA Ops:
  0.0 1.1 %copy-start = (f32[12,13,8,128]{3,2,1,0:T(8,128)S(1)}, f32[12,13,8,128]{3,2,1,0:T(8,128)}, u32[]{:S(2)}) copy-start(f32[12,13,8,128]{3,2,1,0:T(8,128)} %density.1) | copy-start | bytes 1916932
  1.1 0.7 copy-start.1
  19.6 24.1 %collective-permute-start.5 = (f32[4,42,8,128]{3,2,1,0:T(8,128)S(1)}, f32[4,42,8,128]{3,2,1,0:T(8,128)S(1)}, u32[]{:S(2)}, u32[]{:S(2)}) collective-permute-start(f32[4,42,8,128]{3,2,1,0:T(8,128)S(1)} %get-tuple-element.35), channel_id=1, source_target_pairs={{0,8},{1,9},{2,10},{3,11},{4,12},{5,13},{6,14},{7,15},{8,0},{9,1},... | collective-permute-start | bytes 2064392 | tf_op jit(solution)/shard_map/ppermute | solution.py:212
  24.3 21.9 %collective-permute-start.4 = (f32[4,42,8,128]{3,2,1,0:T(8,128)S(1)}, f32[4,42,8,128]{3,2,1,0:T(8,128)S(1)}, u32[]{:S(2)}, u32[]{:S(2)}) collective-permute-start(f32[4,42,8,128]{3,2,1,0:T(8,128)S(1)} %get-tuple-element.35), channel_id=1, source_target_pairs={{0,12},{1,13},{2,14},{3,15},{4,0},{5,1},{6,2},{7,3},{8,4},{9,5},{1... | collective-permute-start | bytes 2064392 | tf_op jit(solution)/shard_map/ppermute | solution.py:212
  27.1 19.2 %collective-permute-start.3 = (f32[4,42,8,128]{3,2,1,0:T(8,128)S(1)}, f32[4,42,8,128]{3,2,1,0:T(8,128)S(1)}, u32[]{:S(2)}, u32[]{:S(2)}) collective-permute-start(f32[4,42,8,128]{3,2,1,0:T(8,128)S(1)} %get-tuple-element.35), channel_id=1, source_target_pairs={{0,4},{1,5},{2,6},{3,7},{4,8},{5,9},{6,10},{7,11},{8,12},{9,13},{1... | collective-permute-start | bytes 2064392 | tf_op jit(solution)/shard_map/ppermute | solution.py:212
  29.6 11.3 %collective-permute-start.6 = (f32[6,13,8,128]{3,2,1,0:T(8,128)S(1)}, f32[6,13,8,128]{3,2,1,0:T(8,128)S(1)}, u32[]{:S(2)}, u32[]{:S(2)}) collective-permute-start(f32[6,13,8,128]{3,2,1,0:T(8,128)S(1)} %get-tuple-element.21.middle.before), channel_id=1, source_target_pairs={{0,496},{1,497},{2,498},{3,499},{4,500},{5,501},{6,502},{7,503},{8... | collective-permute-start | bytes 958472 | tf_op jit(solution)/shard_map/ppermute | solution.py:212
  36.0 29.0 %collective-permute-start.2 = (f32[4,42,8,128]{3,2,1,0:T(8,128)S(1)}, f32[4,42,8,128]{3,2,1,0:T(8,128)S(1)}, u32[]{:S(2)}, u32[]{:S(2)}) collective-permute-start(f32[4,42,8,128]{3,2,1,0:T(8,128)S(1)} %get-tuple-element.36), channel_id=1, source_target_pairs={{0,8},{1,9},{2,10},{3,11},{4,12},{5,13},{6,14},{7,15},{8,0},{9,1},... | collective-permute-start | bytes 2064392 | tf_op jit(solution)/shard_map/ppermute | solution.py:212
  40.9 24.1 %collective-permute-start.1 = (f32[4,42,8,128]{3,2,1,0:T(8,128)S(1)}, f32[4,42,8,128]{3,2,1,0:T(8,128)S(1)}, u32[]{:S(2)}, u32[]{:S(2)}) collective-permute-start(f32[4,42,8,128]{3,2,1,0:T(8,128)S(1)} %get-tuple-element.36), channel_id=1, source_target_pairs={{0,12},{1,13},{2,14},{3,15},{4,0},{5,1},{6,2},{7,3},{8,4},{9,5},{1... | collective-permute-start | bytes 2064392 | tf_op jit(solution)/shard_map/ppermute | solution.py:212
  43.7 21.3 %collective-permute-start = (f32[4,42,8,128]{3,2,1,0:T(8,128)S(1)}, f32[4,42,8,128]{3,2,1,0:T(8,128)S(1)}, u32[]{:S(2)}, u32[]{:S(2)}) collective-permute-start(f32[4,42,8,128]{3,2,1,0:T(8,128)S(1)} %get-tuple-element.36), channel_id=1, source_target_pairs={{0,4},{1,5},{2,6},{3,7},{4,8},{5,9},{6,10},{7,11},{8,12},{9,13},{1... | collective-permute-start | bytes 2064392 | tf_op jit(solution)/shard_map/ppermute | solution.py:212
  49.5 14.5 %collective-permute-start.7 = (f32[3,144,256]{2,1,0:T(8,128)S(1)}, f32[3,144,256]{2,1,0:T(8,128)S(1)}, u32[]{:S(2)}, u32[]{:S(2)}) collective-permute-start(f32[3,144,256]{2,1,0:T(8,128)S(1)} %get-tuple-element.23), channel_id=1, source_target_pairs={{0,496},{1,497},{2,498},{3,499},{4,500},{5,501},{6,502},{7,503},{8... | collective-permute-start | bytes 1327112 | tf_op jit(solution)/shard_map/ppermute | solution.py:212
  57.7 7.3 %collective-permute-start.8 = (f32[6,13,8,128]{3,2,1,0:T(8,128)S(1)}, f32[6,13,8,128]{3,2,1,0:T(8,128)S(1)}, u32[]{:S(2)}, u32[]{:S(2)}) collective-permute-start(f32[6,13,8,128]{3,2,1,0:T(8,128)S(1)} %get-tuple-element.22.after.middle), channel_id=1, source_target_pairs={{0,16},{1,17},{2,18},{3,19},{4,20},{5,21},{6,22},{7,23},{8,24},{9,... | collective-permute-start | bytes 958472 | tf_op jit(solution)/shard_map/ppermute | solution.py:212
  64.0 1.1 %copy-start.2 = (s32[12,13]{1,0:T(8,128)S(1)}, s32[12,13]{1,0:T(8,128)}, u32[]{:S(2)}) copy-start(s32[12,13]{1,0:T(8,128)} %pattern.7) | copy-start | bytes 1876
  68.3 5.4 %collective-permute-start.9 = (f32[3,144,256]{2,1,0:T(8,128)S(1)}, f32[3,144,256]{2,1,0:T(8,128)S(1)}, u32[]{:S(2)}, u32[]{:S(2)}) collective-permute-start(f32[3,144,256]{2,1,0:T(8,128)S(1)} %get-tuple-element.28), channel_id=1, source_target_pairs={{0,16},{1,17},{2,18},{3,19},{4,20},{5,21},{6,22},{7,23},{8,24},{9,... | collective-permute-start | bytes 1327112 | tf_op jit(solution)/shard_map/ppermute | solution.py:212

commit v3 on v2

v3 whole, which is shorter than its diff:
```python
import functools

import jax
import jax.numpy as jnp
from jax import lax
from jax.experimental import pallas as pl
from jax.experimental.pallas import tpu as pltpu
from jax.sharding import PartitionSpec as P

HALF = 6
SLOTS = 13
ONES = 7
COLS = 8
B = 128
CHUNK = HALF * ONES
PAIRS = HALF // 2
VIEW = 14 * COLS
WIDE = 26 * COLS
HALO = 18 * COLS
DEPTH = 14 * B
F32 = jnp.float32
BF16 = jnp.bfloat16
AXES = ("row", "col")


def flipped(core, index, last):
    return jnp.where(core == 0, index, last - index)


def split(value):
    high = value.astype(BF16)
    return high, (value - high.astype(F32)).astype(BF16)


def row_codes(core, pattern):
    lane = lax.broadcasted_iota(jnp.int32, pattern.shape, 1)
    rank = jnp.zeros(pattern.shape, jnp.int32)
    for s in range(SLOTS - 1):
        rank = rank + jnp.where(lane > s, pattern[:, s : s + 1], 0)
    slot = flipped(core, lane, SLOTS - 1)
    rank = flipped(core, rank, ONES - 1)
    return jnp.sum(pattern * lax.shift_left(slot, 4 * rank), axis=1, keepdims=True)


def code_of(codes, core, row):
    return codes[flipped(core, row, 2 * HALF - 1), 0]


def slot_of(code, t):
    return lax.shift_right_logical(code, 4 * t) & 15


def unused_slots(code):
    held = jnp.int32(0)
    for t in range(ONES):
        held = held | lax.shift_left(jnp.int32(1), slot_of(code, t))
    rest, rank = jnp.int32(0), jnp.int32(0)
    for s in range(SLOTS):
        off = 1 - (lax.shift_right_logical(held, s) & 1)
        rest = rest | (off * lax.shift_left(jnp.int32(s), 4 * rank))
        rank = rank + off
    return rest


def prepare(pattern, density, packed, dense0, dense1, codes):
    core = lax.rem(lax.axis_index("row"), 2)
    codes[...] = jnp.broadcast_to(row_codes(core, pattern[...]), codes.shape)
    for u in range(2 * HALF):
        r = flipped(core, u, 2 * HALF - 1)
        code = codes[r, 0]
        dense = (dense0, dense1)[u // HALF]
        for s in range(SLOTS):
            dense[u % HALF, s] = jnp.zeros((COLS, B), F32)
        for t in range(ONES):
            s = slot_of(code, t)
            tile = density[r, flipped(core, s, SLOTS - 1)]
            dense[u % HALF, s] = tile
            for copy in range(4):
                packed[copy, u * ONES + t] = tile


def paired(first, second):
    gap = jnp.zeros((COLS, B), F32)
    return jnp.concatenate(
        [jnp.concatenate([first, gap], axis=0), jnp.concatenate([gap, second], axis=0)], axis=1
    )


def right_operand(chunk, before, middle, after, sides):
    def other_way(ref, v):
        return jnp.concatenate([ref[HALF - 1 - v, SLOTS - 1 - s] for s in range(SLOTS)], axis=0)

    def same_way(ref, v):
        return jnp.concatenate([ref[v, s] for s in range(SLOTS)], axis=0)

    for part, ref in enumerate((before, middle, after)):
        turned = part == (0 if chunk == 0 else 2)
        take = other_way if turned else same_way
        for i in range(PAIRS):
            high, low = split(paired(take(ref, 2 * i), take(ref, 2 * i + 1)))
            sides[part * PAIRS + i, :VIEW] = high
            sides[part * PAIRS + i, VIEW:] = low


def left_operand(chunk, codes, near, far_m, far_p, far_o, w_high, w_low, raw):
    core = lax.rem(lax.axis_index("row"), 2)
    col = lax.axis_index("col")
    y, x = col // 4, lax.rem(col, 4)

    second = jnp.where(core == 0, y, x)
    for ref, base, step in ((near, chunk * CHUNK, 0), (far_m, 0, -1), (far_p, 0, 1), (far_o, 0, 2)):
        other = lax.rem(second + step + 4, 4)
        for i in range(4):
            spot = jnp.where(core == 0, other * 4 + i, i * 4 + other)
            rows = pl.ds(pl.multiple_of(spot * COLS, COLS), COLS)
            for t in range(CHUNK):
                raw[t, rows, :] = ref[i, base + t]

    nothing = jnp.zeros((B, B), BF16)
    for i in range(PAIRS):
        for q in range(2):
            v = 2 * i + q
            code = code_of(codes, core, chunk * HALF + v)
            rest = unused_slots(code)
            lanes = slice(q * B, (q + 1) * B)
            corner = slice((DEPTH - B) * (1 - q), (DEPTH - B) * (1 - q) + B)
            w_high[i, corner, lanes] = nothing
            w_low[i, corner, lanes] = nothing
            for t in range(SLOTS - ONES):
                rows = pl.ds(pl.multiple_of((slot_of(rest, t) + q) * B, B), B)
                w_high[i, rows, lanes] = nothing
                w_low[i, rows, lanes] = nothing
            for t in range(ONES):
                high, low = split(raw[v * ONES + t])
                rows = pl.ds(pl.multiple_of((slot_of(code, t) + q) * B, B), B)
                w_high[i, rows, lanes] = high
                w_low[i, rows, lanes] = low


def squares(chunk, sides, w_high, w_low, square, halo):
    for i in range(PAIRS):
        square[i] = jnp.zeros((WIDE, 2 * B), F32)
        for m in range(7):
            depth = slice(m * 2 * B, (m + 1) * 2 * B)
            whole = jnp.dot(sides[i + m], w_high[i, depth], preferred_element_type=F32)
            small = jnp.dot(sides[i + m, :VIEW], w_low[i, depth], preferred_element_type=F32)
            square[i, 2 * COLS * m : 2 * COLS * m + VIEW] += whole[:VIEW] + whole[VIEW:] + small
        if chunk == 0:
            halo[i] = square[i, :HALO]
        else:
            halo[i] = square[i, WIDE - HALO :]


def square_kernel(chunk, codes, near, far_m, far_p, far_o, before, middle, after,
                  square, halo, w_high, w_low, raw, sides):
    right_operand(chunk, before, middle, after, sides)
    left_operand(chunk, codes, near, far_m, far_p, far_o, w_high, w_low, raw)
    squares(chunk, sides, w_high, w_low, square, halo)


def lift(ref, held):
    for i in range(PAIRS):
        held[0, i], held[1, i] = split(ref[i])


def lift_halo(ref, held, first):
    for i in range(PAIRS):
        source = ref[PAIRS - 1 - i]
        turned = jnp.concatenate(
            [source[(HALO // COLS - 1 - j) * COLS : (HALO // COLS - j) * COLS] for j in range(HALO // COLS)], axis=0
        )
        turned = jnp.concatenate([turned[:, B:], turned[:, :B]], axis=1)
        held[0, i, first : first + HALO], held[1, i, first : first + HALO] = split(turned)


def add_products(total, held, part, w_high, w_low):
    for i in range(PAIRS):
        value = None
        for k in range(PAIRS):
            m = part * PAIRS + k - i
            if m < 0 or m > 6:
                continue
            rows = slice(2 * COLS * (6 - m), 2 * COLS * (6 - m) + VIEW)
            depth = slice(m * 2 * B, (m + 1) * 2 * B)
            high, low = held[0, k, rows], held[1, k, rows]
            term = (
                jnp.dot(high, w_high[i, depth], preferred_element_type=F32)
                + jnp.dot(low, w_high[i, depth], preferred_element_type=F32)
                + jnp.dot(high, w_low[i, depth], preferred_element_type=F32)
            )
            value = term if value is None else value + term
        total[i] += value


def third_inner(square0, w_high0, w_low0, total0, held0):
    lift(square0, held0)
    total0[...] = jnp.zeros_like(total0)
    add_products(total0, held0, 1, w_high0, w_low0)


def third_second(held0, square1, w_high0, w_low0, w_high1, w_low1, before, total0, total1, held1):
    lift(square1, held1)
    total0[...] = before[...]
    total1[...] = jnp.zeros_like(total1)
    add_products(total0, held1, 2, w_high0, w_low0)
    add_products(total1, held0, 0, w_high1, w_low1)
    add_products(total1, held1, 1, w_high1, w_low1)


def third_outer(halo, w_high0, w_low0, before, total0, held):
    total0[...] = before[...]
    lift_halo(halo, held, WIDE - HALO)
    add_products(total0, held, 0, w_high0, w_low0)


def finish(codes, halo, square0, square1, w_high1, w_low1, total0, before1, out, total1, held):
    core = lax.rem(lax.axis_index("row"), 2)
    lift_halo(halo, held, 0)
    total1[...] = before1[...]
    add_products(total1, held, 2, w_high1, w_low1)
    for chunk, (square, total) in enumerate(((square0, total0), (square1, total1))):
        for i in range(PAIRS):
            value = 3.0 * square[i, 6 * COLS : 6 * COLS + VIEW] - 2.0 * total[i]
            for q in range(2):
                r = flipped(core, chunk * HALF + 2 * i + q, 2 * HALF - 1)
                rest = unused_slots(codes[r, 0])
                for s in range(SLOTS):
                    out[r, flipped(core, s, SLOTS - 1)] = value[(s + q) * COLS : (s + q + 1) * COLS, q * B : (q + 1) * B]
                for t in range(SLOTS - ONES):
                    out[r, flipped(core, slot_of(rest, t), SLOTS - 1)] = jnp.zeros((COLS, B), F32)


VMEM = pl.BlockSpec(memory_space=pltpu.VMEM)
PARAMS = pltpu.CompilerParams(vmem_limit_bytes=16 * 1024 * 1024)


def cost(products):
    flops = 2 * products * 3 * VIEW * 256 * 256
    return pl.CostEstimate(flops=flops, bytes_accessed=4_000_000, transcendentals=0)


def shape(*dims, dtype=F32):
    return jax.ShapeDtypeStruct(dims, dtype)


def shards(density, pattern):
    spots = [(z, c, y, x) for z in range(16) for c in range(2) for y in range(4) for x in range(4)]

    def number(z, c, y, x):
        return (z % 16 * 2 + c) * 16 + y % 4 * 4 + x % 4

    def send(value, move):
        return lax.ppermute(value, AXES, [(number(*spot), number(*move(*spot))) for spot in spots])

    def second_way(step):
        return lambda z, c, y, x: (z, c, y + step, x) if c == 0 else (z, c, y, x + step)

    def next_chip(z, c, y, x):
        return (z - 1, 1, y, x) if c == 0 else (z + 1, 0, y, x)

    def other_core(z, c, y, x):
        return (z, 1 - c, y, x)

    dense_shape = shape(HALF, SLOTS, COLS, B)
    packed, dense0, dense1, codes = pl.pallas_call(
        prepare,
        out_shape=(shape(4, 2 * CHUNK, COLS, B), dense_shape, dense_shape, shape(2 * HALF, B, dtype=jnp.int32)),
        in_specs=[VMEM, VMEM],
        out_specs=(VMEM,) * 4,
        compiler_params=PARAMS,
        name="prepare",
    )(pattern, density)

    quads = []
    for z in range(16):
        for i in range(4):
            quads.append([number(z, 0, i, x) for x in range(4)])
            quads.append([number(z, 1, y, i) for y in range(4)])
    near = lax.all_to_all(packed, AXES, 0, 0, axis_index_groups=quads)
    far = []
    for chunk in range(2):
        part = near[:, chunk * CHUNK : (chunk + 1) * CHUNK]
        far.append([send(part, second_way(step)) for step in (1, -1, 2)])
    halo_z = send(dense0, next_chip)
    weights = shape(PAIRS, DEPTH, 2 * B, dtype=BF16)

    def squared(chunk, *sides):
        return pl.pallas_call(
            functools.partial(square_kernel, chunk),
            out_shape=(shape(PAIRS, WIDE, 2 * B), shape(PAIRS, HALO, 2 * B), weights, weights),
            in_specs=[VMEM] * 8,
            out_specs=(VMEM,) * 4,
            scratch_shapes=[pltpu.VMEM((CHUNK, B, B), F32), pltpu.VMEM((3 * PAIRS, 2 * VIEW, 2 * B), BF16)],
            compiler_params=PARAMS,
            cost_estimate=cost(21),
            name=f"square{chunk}",
        )(codes, near, *far[chunk], *sides)

    square0, edge0, w_high0, w_low0 = squared(0, halo_z, dense0, dense1)
    square_z = send(edge0, next_chip)
    totals = shape(PAIRS, VIEW, 2 * B)
    held_shape = (2, PAIRS, WIDE, 2 * B)
    held = pltpu.VMEM(held_shape, BF16)
    total0, held0 = pl.pallas_call(
        third_inner,
        out_shape=(totals, shape(*held_shape, dtype=BF16)),
        in_specs=[VMEM] * 3,
        out_specs=(VMEM, VMEM),
        compiler_params=PARAMS,
        cost_estimate=cost(9),
        name="third_inner",
    )(square0, w_high0, w_low0)
    dense1_later, far[1][2] = lax.optimization_barrier((dense1, far[1][2]))
    halo_c = send(dense1_later, other_core)
    halo_c, held0 = lax.optimization_barrier((halo_c, held0))
    square1, edge1, w_high1, w_low1 = squared(1, dense0, dense1, halo_c)
    square_c = send(edge1, other_core)
    total0, total1 = pl.pallas_call(
        third_second,
        out_shape=(totals, totals),
        in_specs=[VMEM] * 7,
        out_specs=(VMEM, VMEM),
        scratch_shapes=[held],
        compiler_params=PARAMS,
        cost_estimate=cost(21),
        name="third_second",
    )(held0, square1, w_high0, w_low0, w_high1, w_low1, total0)
    square_z, total0 = lax.optimization_barrier((square_z, total0))
    total0 = pl.pallas_call(
        third_outer,
        out_shape=totals,
        in_specs=[VMEM] * 4,
        out_specs=VMEM,
        scratch_shapes=[held],
        compiler_params=PARAMS,
        cost_estimate=cost(6),
        name="third_outer",
    )(square_z, w_high0, w_low0, total0)
    return pl.pallas_call(
        finish,
        out_shape=shape(2 * HALF, SLOTS, COLS, B),
        in_specs=[VMEM] * 8,
        out_specs=VMEM,
        scratch_shapes=[pltpu.VMEM((PAIRS, VIEW, 2 * B), F32), held],
        compiler_params=PARAMS,
        cost_estimate=cost(6),
        name="finish",
    )(codes, square_c, square0, square1, w_high1, w_low1, total0, total1)


def solution(mesh):
    placed = (P("row", None, "col", None), P("row", None))
    return jax.shard_map(
        shards, mesh=mesh, in_specs=placed, out_specs=P("row", None, "col", None), check_vma=False
    )
```

time: 76.3 us -> 70.4 us (0.923)
  waiting for transfers between devices: 4.33 us -> 0.03 us
  Pallas kernels: 12.4 us -> 9.7 us
  starting transfers between devices: 40.7 us -> 41.8 us
    ppermute x10, waiting for transfers between devices: 4.33 us -> 0.03 us  [send(): lax.ppermute(value, AXES, [(number(*spot), number(*move(*spot))) for spot...]
    pallas_call x2, Pallas kernels: 6.49 us -> 4.95 us  [squared(): pl.pallas_call(functools.partial(square_kernel, chunk), out_shape=(shape(...]
    ppermute x10, starting transfers between devices: 40.7 us -> 41.8 us  [send(): lax.ppermute(value, AXES, [(number(*spot), number(*move(*spot))) for spot...]
    pallas_call x2 -> x3, Pallas kernels: 2.44 us -> 1.59 us  [the longest x1 0.66 us: shards(): pl.pallas_call(third_inner, out_shape=(totals, shape(*held_shape, dtype=B...]
    unnamed x6 -> x4, local copies, waits for them, and re-layouts: 1.78 us -> 1.78 us
  transfers between devices with their start and end apart: 10 -> 10, of which waited for: 2 -> 0; matrix products, arithmetic and copies ran while one was open for 0% -> 0% of each run, Pallas kernels for 7% -> 11%
where the time goes in v3:
time: 70.4 us; the launch traced here: 69.9 us
  starting transfers between devices  41.8 us (59%)
  blocking collectives  16.3 us (23%)
  Pallas kernels  9.7 us (14%)
  local copies, waits for them, and re-layouts  1.87 us (3%)
    ppermute x10, starting transfers between devices, send(): lax.ppermute(value, AXES, [(number(*spot), number(*move(*spot))) for spot...  41.8 us
    all_to_all x1, blocking collectives, shards(): near = lax.all_to_all(packed, AXES, 0, 0, axis_index_groups=quads)  16.3 us
    pallas_call x2, Pallas kernels, squared(): pl.pallas_call(functools.partial(square_kernel, chunk), out_shape=(shape(...  4.95 us
    pallas_call x1, Pallas kernels, shards(): pl.pallas_call(finish, out_shape=shape(2 * HALF, SLOTS, COLS, B), in_spec...  1.79 us
    unnamed x4, local copies, waits for them, and re-layouts  1.78 us
  transfers between devices with their start and end apart: 10, of which 0 were waited for; matrix products, arithmetic and copies ran while one was open for 0% of the time, Pallas kernels for 11%

profile of v3, /device:TPU:1, one launch (start us, length us, event | category | flops | bytes accessed | tf_op | source)
XLA Modules:
  0.0 69.9 jit_solution(5192578894811331455)
XLA Ops:
  0.0 0.0 copy-start
  0.0 1.1 %copy-done = f32[12,13,8,128]{3,2,1,0:T(8,128)S(1)} copy-done((f32[12,13,8,128]{3,2,1,0:T(8,128)S(1)}, f32[12,13,8,128]{3,2,1,0:T(8,128)}, u32[]{:S(2)}) %copy-start) | copy-done | bytes 639000
  1.1 0.0 copy-start.1
  1.1 0.7 copy-done.1
  1.8 0.5 prepare.1
  2.2 16.3 %all_to_all.5.near = f32[4,84,8,128]{3,2,1,0:T(8,128)S(1)} all-to-all(f32[4,84,8,128]{3,2,1,0:T(8,128)S(1)} %get-tuple-element.28), channel_id=1, replica_groups={{0,1,2,3},{16,20,24,28},{4,5,6,7},{17,21,25,29},{8,9,10,11},{18,22,26,3..., dimensions={0} | all-to-all | bytes 2752512 | tf_op jit(solution)/shard_map/all_to_all | solution.py:279
  18.6 0.1 fusion
  18.6 4.7 %collective-permute-start.2 = (f32[4,42,8,128]{3,2,1,0:T(8,128)S(1)}, f32[4,42,8,128]{3,2,1,0:T(8,128)S(1)}, u32[]{:S(2)}, u32[]{:S(2)}) collective-permute-start(f32[4,42,8,128]{3,2,1,0:T(8,128)S(1)} %get-tuple-element.50), channel_id=1, source_target_pairs={{0,8},{1,9},{2,10},{3,11},{4,12},{5,13},{6,14},{7,15},{8,0},{9,1},... | collective-permute-start | bytes 2064392 | tf_op jit(solution)/shard_map/ppermute | solution.py:253
  23.3 2.1 %collective-permute-start.6 = (f32[4,42,8,128]{3,2,1,0:T(8,128)S(1)}, f32[4,42,8,128]{3,2,1,0:T(8,128)S(1)}, u32[]{:S(2)}, u32[]{:S(2)}) collective-permute-start(f32[4,42,8,128]{3,2,1,0:T(8,128)S(1)} %get-tuple-element.49), channel_id=1, source_target_pairs={{0,8},{1,9},{2,10},{3,11},{4,12},{5,13},{6,14},{7,15},{8,0},{9,1},... | collective-permute-start | bytes 2064392 | tf_op jit(solution)/shard_map/ppermute | solution.py:253
  25.4 5.9 %collective-permute-start.7 = (f32[6,13,8,128]{3,2,1,0:T(8,128)S(1)}, f32[6,13,8,128]{3,2,1,0:T(8,128)S(1)}, u32[]{:S(2)}, u32[]{:S(2)}) collective-permute-start(f32[6,13,8,128]{3,2,1,0:T(8,128)S(1)} %get-tuple-element.31.middle.before), channel_id=1, source_target_pairs={{0,496},{1,497},{2,498},{3,499},{4,500},{5,501},{6,502},{7,503},{8... | collective-permute-start | bytes 958472 | tf_op jit(solution)/shard_map/ppermute | solution.py:253
  31.4 2.8 %collective-permute-start.5 = (f32[4,42,8,128]{3,2,1,0:T(8,128)S(1)}, f32[4,42,8,128]{3,2,1,0:T(8,128)S(1)}, u32[]{:S(2)}, u32[]{:S(2)}) collective-permute-start(f32[4,42,8,128]{3,2,1,0:T(8,128)S(1)} %get-tuple-element.49), channel_id=1, source_target_pairs={{0,12},{1,13},{2,14},{3,15},{4,0},{5,1},{6,2},{7,3},{8,4},{9,5},{1... | collective-permute-start | bytes 2064392 | tf_op jit(solution)/shard_map/ppermute | solution.py:253
  34.2 2.5 %collective-permute-start.4 = (f32[4,42,8,128]{3,2,1,0:T(8,128)S(1)}, f32[4,42,8,128]{3,2,1,0:T(8,128)S(1)}, u32[]{:S(2)}, u32[]{:S(2)}) collective-permute-start(f32[4,42,8,128]{3,2,1,0:T(8,128)S(1)} %get-tuple-element.49), channel_id=1, source_target_pairs={{0,4},{1,5},{2,6},{3,7},{4,8},{5,9},{6,10},{7,11},{8,12},{9,13},{1... | collective-permute-start | bytes 2064392 | tf_op jit(solution)/shard_map/ppermute | solution.py:253
  36.7 0.0 collective-permute-done.7.before
  36.7 4.0 %collective-permute-start.1 = (f32[4,42,8,128]{3,2,1,0:T(8,128)S(1)}, f32[4,42,8,128]{3,2,1,0:T(8,128)S(1)}, u32[]{:S(2)}, u32[]{:S(2)}) collective-permute-start(f32[4,42,8,128]{3,2,1,0:T(8,128)S(1)} %get-tuple-element.50), channel_id=1, source_target_pairs={{0,12},{1,13},{2,14},{3,15},{4,0},{5,1},{6,2},{7,3},{8,4},{9,5},{1... | collective-permute-start | bytes 2064392 | tf_op jit(solution)/shard_map/ppermute | solution.py:253
  40.7 0.0 collective-permute-done.2.far_o
  40.7 1.9 %collective-permute-start = (f32[4,42,8,128]{3,2,1,0:T(8,128)S(1)}, f32[4,42,8,128]{3,2,1,0:T(8,128)S(1)}, u32[]{:S(2)}, u32[]{:S(2)}) collective-permute-start(f32[4,42,8,128]{3,2,1,0:T(8,128)S(1)} %get-tuple-element.50), channel_id=1, source_target_pairs={{0,4},{1,5},{2,6},{3,7},{4,8},{5,9},{6,10},{7,11},{8,12},{9,13},{1... | collective-permute-start | bytes 2064392 | tf_op jit(solution)/shard_map/ppermute | solution.py:253
  42.6 0.0 collective-permute-done.6.far_o
  42.7 8.6 %collective-permute-start.3 = (f32[6,13,8,128]{3,2,1,0:T(8,128)S(1)}, f32[6,13,8,128]{3,2,1,0:T(8,128)S(1)}, u32[]{:S(2)}, u32[]{:S(2)}) collective-permute-start(f32[6,13,8,128]{3,2,1,0:T(8,128)S(1)} %get-tuple-element.32.after.middle), channel_id=1, source_target_pairs={{0,16},{1,17},{2,18},{3,19},{4,20},{5,21},{6,22},{7,23},{8,24},{9,... | collective-permute-start | bytes 958472 | tf_op jit(solution)/shard_map/ppermute | solution.py:253
  51.2 0.0 collective-permute-done.5.far_p
  51.2 0.0 collective-permute-done.4.far_m
  51.2 2.5 %square0.1 = (f32[3,208,256]{2,1,0:T(8,128)S(1)}, f32[3,144,256]{2,1,0:T(8,128)S(1)}, bf16[3,1792,256]{2,1,0:T(8,128)(2,1)S(1)}, bf16[3,1792,256]{2,1,0:T(8,128)(2,1)S(1)}) custom-call(s32[12,128]{1,0:T(8,128)S(1)} %get-tuple-element.27.codes, f32[4,84,8,128]{3,2,1,0:T(8,128)S(1)} %all_to_all.5.near, f32[4,42,8,128]{3,2,1,0:T(8,128)S(1)} %collective-permute-done.4.far_m, ...), custom_call_target="tpu_custom_call" | custom-call | flops 924844032 | bytes 4000000 | tf_op jit(solution)/shard_map/square0/pallas_call | solution.py:288
  53.7 2.2 %collective-permute-start.9 = (f32[3,144,256]{2,1,0:T(8,128)S(1)}, f32[3,144,256]{2,1,0:T(8,128)S(1)}, u32[]{:S(2)}, u32[]{:S(2)}) collective-permute-start(f32[3,144,256]{2,1,0:T(8,128)S(1)} %get-tuple-element.42), channel_id=1, source_target_pairs={{0,496},{1,497},{2,498},{3,499},{4,500},{5,501},{6,502},{7,503},{8... | collective-permute-start | bytes 1327112 | tf_op jit(solution)/shard_map/ppermute | solution.py:253
  55.9 0.7 third_inner.1
  56.6 0.0 collective-permute-done.3.after
  56.6 0.0 collective-permute-done.1.far_p
  56.6 0.0 collective-permute-done.far_m
  56.6 2.5 %square1.1 = (f32[3,208,256]{2,1,0:T(8,128)S(1)}, f32[3,144,256]{2,1,0:T(8,128)S(1)}, bf16[3,1792,256]{2,1,0:T(8,128)(2,1)S(1)}, bf16[3,1792,256]{2,1,0:T(8,128)(2,1)S(1)}) custom-call(s32[12,128]{1,0:T(8,128)S(1)} %get-tuple-element.27.codes, f32[4,84,8,128]{3,2,1,0:T(8,128)S(1)} %all_to_all.5.near, f32[4,42,8,128]{3,2,1,0:T(8,128)S(1)} %collective-permute-done.far_m, ...), custom_call_target="tpu_custom_call" | custom-call | flops 924844032 | bytes 4000000 | tf_op jit(solution)/shard_map/square1/pallas_call | solution.py:288
  59.1 7.1 %collective-permute-start.8 = (f32[3,144,256]{2,1,0:T(8,128)S(1)}, f32[3,144,256]{2,1,0:T(8,128)S(1)}, u32[]{:S(2)}, u32[]{:S(2)}) collective-permute-start(f32[3,144,256]{2,1,0:T(8,128)S(1)} %get-tuple-element.38), channel_id=1, source_target_pairs={{0,16},{1,17},{2,18},{3,19},{4,20},{5,21},{6,22},{7,23},{8,24},{9,... | collective-permute-start | bytes 1327112 | tf_op jit(solution)/shard_map/ppermute | solution.py:253
  66.2 1.4 %third_second.1 = (f32[3,112,256]{2,1,0:T(8,128)S(1)}, f32[3,112,256]{2,1,0:T(8,128)S(1)}) custom-call(bf16[2,3,208,256]{3,2,1,0:T(8,128)(2,1)S(1)} %get-tuple-element.43.held0, f32[3,208,256]{2,1,0:T(8,128)S(1)} %get-tuple-element.39.square1, bf16[3,1792,256]{2,1,0:T(8,128)(2,1)S(1)} %get-tuple-element.34.w_high0, ...), custom_call_target="tpu_custom_call" | custom-call | flops 924844032 | bytes 4000000 | tf_op jit(solution)/shard_map/third_second/pallas_call | solution.py:318
  67.6 0.0 collective-permute-done.9.halo
  67.6 0.5 third_outer.1.total0
  68.1 0.0 collective-permute-done.8.halo
  68.1 1.8 %finish.1 = f32[12,13,8,128]{3,2,1,0:T(8,128)} custom-call(s32[12,128]{1,0:T(8,128)S(1)} %get-tuple-element.27.codes, f32[3,144,256]{2,1,0:T(8,128)S(1)} %collective-permute-done.8.halo, f32[3,208,256]{2,1,0:T(8,128)S(1)} %get-tuple-element.33.square0, f32[3,208,256]{2,1,0:T(8,128)S(1)} %get-tuple-element.39.square1, ...), custom_call_target="tpu_custom_call" | custom-call | flops 264241152 | bytes 4000000 | tf_op jit(solution)/shard_map/finish/pallas_call | solution.py:339
Async XLA Ops:
  0.0 1.1 %copy-start = (f32[12,13,8,128]{3,2,1,0:T(8,128)S(1)}, f32[12,13,8,128]{3,2,1,0:T(8,128)}, u32[]{:S(2)}) copy-start(f32[12,13,8,128]{3,2,1,0:T(8,128)} %density.1) | copy-start | bytes 1916932
  1.1 0.7 copy-start.1
  18.6 22.1 %collective-permute-start.2 = (f32[4,42,8,128]{3,2,1,0:T(8,128)S(1)}, f32[4,42,8,128]{3,2,1,0:T(8,128)S(1)}, u32[]{:S(2)}, u32[]{:S(2)}) collective-permute-start(f32[4,42,8,128]{3,2,1,0:T(8,128)S(1)} %get-tuple-element.50), channel_id=1, source_target_pairs={{0,8},{1,9},{2,10},{3,11},{4,12},{5,13},{6,14},{7,15},{8,0},{9,1},... | collective-permute-start | bytes 2064392 | tf_op jit(solution)/shard_map/ppermute | solution.py:253
  23.3 19.3 %collective-permute-start.6 = (f32[4,42,8,128]{3,2,1,0:T(8,128)S(1)}, f32[4,42,8,128]{3,2,1,0:T(8,128)S(1)}, u32[]{:S(2)}, u32[]{:S(2)}) collective-permute-start(f32[4,42,8,128]{3,2,1,0:T(8,128)S(1)} %get-tuple-element.49), channel_id=1, source_target_pairs={{0,8},{1,9},{2,10},{3,11},{4,12},{5,13},{6,14},{7,15},{8,0},{9,1},... | collective-permute-start | bytes 2064392 | tf_op jit(solution)/shard_map/ppermute | solution.py:253
  25.4 11.2 %collective-permute-start.7 = (f32[6,13,8,128]{3,2,1,0:T(8,128)S(1)}, f32[6,13,8,128]{3,2,1,0:T(8,128)S(1)}, u32[]{:S(2)}, u32[]{:S(2)}) collective-permute-start(f32[6,13,8,128]{3,2,1,0:T(8,128)S(1)} %get-tuple-element.31.middle.before), channel_id=1, source_target_pairs={{0,496},{1,497},{2,498},{3,499},{4,500},{5,501},{6,502},{7,503},{8... | collective-permute-start | bytes 958472 | tf_op jit(solution)/shard_map/ppermute | solution.py:253
  31.4 19.8 %collective-permute-start.5 = (f32[4,42,8,128]{3,2,1,0:T(8,128)S(1)}, f32[4,42,8,128]{3,2,1,0:T(8,128)S(1)}, u32[]{:S(2)}, u32[]{:S(2)}) collective-permute-start(f32[4,42,8,128]{3,2,1,0:T(8,128)S(1)} %get-tuple-element.49), channel_id=1, source_target_pairs={{0,12},{1,13},{2,14},{3,15},{4,0},{5,1},{6,2},{7,3},{8,4},{9,5},{1... | collective-permute-start | bytes 2064392 | tf_op jit(solution)/shard_map/ppermute | solution.py:253
  34.2 17.1 %collective-permute-start.4 = (f32[4,42,8,128]{3,2,1,0:T(8,128)S(1)}, f32[4,42,8,128]{3,2,1,0:T(8,128)S(1)}, u32[]{:S(2)}, u32[]{:S(2)}) collective-permute-start(f32[4,42,8,128]{3,2,1,0:T(8,128)S(1)} %get-tuple-element.49), channel_id=1, source_target_pairs={{0,4},{1,5},{2,6},{3,7},{4,8},{5,9},{6,10},{7,11},{8,12},{9,13},{1... | collective-permute-start | bytes 2064392 | tf_op jit(solution)/shard_map/ppermute | solution.py:253
  36.7 19.9 %collective-permute-start.1 = (f32[4,42,8,128]{3,2,1,0:T(8,128)S(1)}, f32[4,42,8,128]{3,2,1,0:T(8,128)S(1)}, u32[]{:S(2)}, u32[]{:S(2)}) collective-permute-start(f32[4,42,8,128]{3,2,1,0:T(8,128)S(1)} %get-tuple-element.50), channel_id=1, source_target_pairs={{0,12},{1,13},{2,14},{3,15},{4,0},{5,1},{6,2},{7,3},{8,4},{9,5},{1... | collective-permute-start | bytes 2064392 | tf_op jit(solution)/shard_map/ppermute | solution.py:253
  40.7 15.9 %collective-permute-start = (f32[4,42,8,128]{3,2,1,0:T(8,128)S(1)}, f32[4,42,8,128]{3,2,1,0:T(8,128)S(1)}, u32[]{:S(2)}, u32[]{:S(2)}) collective-permute-start(f32[4,42,8,128]{3,2,1,0:T(8,128)S(1)} %get-tuple-element.50), channel_id=1, source_target_pairs={{0,4},{1,5},{2,6},{3,7},{4,8},{5,9},{6,10},{7,11},{8,12},{9,13},{1... | collective-permute-start | bytes 2064392 | tf_op jit(solution)/shard_map/ppermute | solution.py:253
  42.7 13.9 %collective-permute-start.3 = (f32[6,13,8,128]{3,2,1,0:T(8,128)S(1)}, f32[6,13,8,128]{3,2,1,0:T(8,128)S(1)}, u32[]{:S(2)}, u32[]{:S(2)}) collective-permute-start(f32[6,13,8,128]{3,2,1,0:T(8,128)S(1)} %get-tuple-element.32.after.middle), channel_id=1, source_target_pairs={{0,16},{1,17},{2,18},{3,19},{4,20},{5,21},{6,22},{7,23},{8,24},{9,... | collective-permute-start | bytes 958472 | tf_op jit(solution)/shard_map/ppermute | solution.py:253
  53.7 13.9 %collective-permute-start.9 = (f32[3,144,256]{2,1,0:T(8,128)S(1)}, f32[3,144,256]{2,1,0:T(8,128)S(1)}, u32[]{:S(2)}, u32[]{:S(2)}) collective-permute-start(f32[3,144,256]{2,1,0:T(8,128)S(1)} %get-tuple-element.42), channel_id=1, source_target_pairs={{0,496},{1,497},{2,498},{3,499},{4,500},{5,501},{6,502},{7,503},{8... | collective-permute-start | bytes 1327112 | tf_op jit(solution)/shard_map/ppermute | solution.py:253
  59.1 9.0 %collective-permute-start.8 = (f32[3,144,256]{2,1,0:T(8,128)S(1)}, f32[3,144,256]{2,1,0:T(8,128)S(1)}, u32[]{:S(2)}, u32[]{:S(2)}) collective-permute-start(f32[3,144,256]{2,1,0:T(8,128)S(1)} %get-tuple-element.38), channel_id=1, source_target_pairs={{0,16},{1,17},{2,18},{3,19},{4,20},{5,21},{6,22},{7,23},{8,24},{9,... | collective-permute-start | bytes 1327112 | tf_op jit(solution)/shard_map/ppermute | solution.py:253

commit v4 on v3

--- a/solution.py
+++ b/solution.py
@@ -62,9 +62,15 @@
     return rest
 
 
-def prepare(pattern, density, packed, dense0, dense1, codes):
+def prepare(pattern_far, density_far, packed, dense0, dense1, codes, pattern, density, sems):
     core = lax.rem(lax.axis_index("row"), 2)
+    get_pattern = pltpu.make_async_copy(pattern_far, pattern, sems.at[0])
+    get_density = pltpu.make_async_copy(density_far, density, sems.at[1])
+    get_pattern.start()
+    get_density.start()
+    get_pattern.wait()
     codes[...] = jnp.broadcast_to(row_codes(core, pattern[...]), codes.shape)
+    get_density.wait()
     for u in range(2 * HALF):
         r = flipped(core, u, 2 * HALF - 1)
         code = codes[r, 0]
@@ -102,7 +108,7 @@
             sides[part * PAIRS + i, VIEW:] = low
 
 
-def left_operand(chunk, codes, near, far_m, far_p, far_o, w_high, w_low, raw):
+def collect_left(chunk, near, far_m, far_p, far_o, raw):
     core = lax.rem(lax.axis_index("row"), 2)
     col = lax.axis_index("col")
     y, x = col // 4, lax.rem(col, 4)
@@ -116,46 +122,51 @@
             for t in range(CHUNK):
                 raw[t, rows, :] = ref[i, base + t]
 
+
+def left_operand(codes, chunk, i, raw, w_high, w_low):
+    core = lax.rem(lax.axis_index("row"), 2)
     nothing = jnp.zeros((B, B), BF16)
+    for q in range(2):
+        v = 2 * i + q
+        code = code_of(codes, core, chunk * HALF + v)
+        rest = unused_slots(code)
+        lanes = slice(q * B, (q + 1) * B)
+        corner = slice((DEPTH - B) * (1 - q), (DEPTH - B) * (1 - q) + B)
+        w_high[corner, lanes] = nothing
+        w_low[corner, lanes] = nothing
+        for t in range(SLOTS - ONES):
+            rows = pl.ds(pl.multiple_of((slot_of(rest, t) + q) * B, B), B)
+            w_high[rows, lanes] = nothing
+            w_low[rows, lanes] = nothing
+        for t in range(ONES):
+            high, low = split(raw[v * ONES + t])
+            rows = pl.ds(pl.multiple_of((slot_of(code, t) + q) * B, B), B)
+            w_high[rows, lanes] = high
+            w_low[rows, lanes] = low
+
+
+def squares(chunk, i, sides, w_high, w_low, square, halo):
+    square[i] = jnp.zeros((WIDE, 2 * B), F32)
+    for m in range(7):
+        depth = slice(m * 2 * B, (m + 1) * 2 * B)
+        whole = jnp.dot(sides[i + m], w_high[depth], preferred_element_type=F32)
+        small = jnp.dot(sides[i + m, :VIEW], w_low[depth], preferred_element_type=F32)
+        square[i, 2 * COLS * m : 2 * COLS * m + VIEW] += whole[:VIEW] + whole[VIEW:] + small
+    if chunk == 0:
+        halo[i] = square[i, :HALO]
+    else:
+        halo[i] = square[i, WIDE - HALO :]
+
+
+def square_kernel(chunk, codes, near, far_m, far_p, far_o, before, middle, after, square, halo, *rest):
+    w_high, w_low, (raw, sides) = rest[:PAIRS], rest[PAIRS : 2 * PAIRS], rest[2 * PAIRS :]
+    collect_left(chunk, near, far_m, far_p, far_o, raw)
+    right_operand(chunk, before, middle, after, sides)
+    left_operand(codes, chunk, 0, raw, w_high[0], w_low[0])
     for i in range(PAIRS):
-        for q in range(2):
-            v = 2 * i + q
-            code = code_of(codes, core, chunk * HALF + v)
-            rest = unused_slots(code)
-            lanes = slice(q * B, (q + 1) * B)
-            corner = slice((DEPTH - B) * (1 - q), (DEPTH - B) * (1 - q) + B)
-            w_high[i, corner, lanes] = nothing
-            w_low[i, corner, lanes] = nothing
-            for t in range(SLOTS - ONES):
-                rows = pl.ds(pl.multiple_of((slot_of(rest, t) + q) * B, B), B)
-                w_high[i, rows, lanes] = nothing
-                w_low[i, rows, lanes] = nothing
-            for t in range(ONES):
-                high, low = split(raw[v * ONES + t])
-                rows = pl.ds(pl.multiple_of((slot_of(code, t) + q) * B, B), B)
-                w_high[i, rows, lanes] = high
-                w_low[i, rows, lanes] = low
-
-
-def squares(chunk, sides, w_high, w_low, square, halo):
-    for i in range(PAIRS):
-        square[i] = jnp.zeros((WIDE, 2 * B), F32)
-        for m in range(7):
-            depth = slice(m * 2 * B, (m + 1) * 2 * B)
-            whole = jnp.dot(sides[i + m], w_high[i, depth], preferred_element_type=F32)
-            small = jnp.dot(sides[i + m, :VIEW], w_low[i, depth], preferred_element_type=F32)
-            square[i, 2 * COLS * m : 2 * COLS * m + VIEW] += whole[:VIEW] + whole[VIEW:] + small
-        if chunk == 0:
-            halo[i] = square[i, :HALO]
-        else:
-            halo[i] = square[i, WIDE - HALO :]
-
-
-def square_kernel(chunk, codes, near, far_m, far_p, far_o, before, middle, after,
-                  square, halo, w_high, w_low, raw, sides):
-    right_operand(chunk, before, middle, after, sides)
-    left_operand(chunk, codes, near, far_m, far_p, far_o, w_high, w_low, raw)
-    squares(chunk, sides, w_high, w_low, square, halo)
+        if i + 1 < PAIRS:
+            left_operand(codes, chunk, i + 1, raw, w_high[i + 1], w_low[i + 1])
+        squares(chunk, i, sides, w_high[i], w_low[i], square, halo)
 
 
 def lift(ref, held):
@@ -184,21 +195,24 @@
             depth = slice(m * 2 * B, (m + 1) * 2 * B)
             high, low = held[0, k, rows], held[1, k, rows]
             term = (
-                jnp.dot(high, w_high[i, depth], preferred_element_type=F32)
-                + jnp.dot(low, w_high[i, depth], preferred_element_type=F32)
-                + jnp.dot(high, w_low[i, depth], preferred_element_type=F32)
+                jnp.dot(high, w_high[i][depth], preferred_element_type=F32)
+                + jnp.dot(low, w_high[i][depth], preferred_element_type=F32)
+                + jnp.dot(high, w_low[i][depth], preferred_element_type=F32)
             )
             value = term if value is None else value + term
         total[i] += value
 
 
-def third_inner(square0, w_high0, w_low0, total0, held0):
+def third_inner(square0, *rest):
+    w_high0, w_low0, (total0, held0) = rest[:PAIRS], rest[PAIRS : 2 * PAIRS], rest[2 * PAIRS :]
     lift(square0, held0)
     total0[...] = jnp.zeros_like(total0)
     add_products(total0, held0, 1, w_high0, w_low0)
 
 
-def third_second(held0, square1, w_high0, w_low0, w_high1, w_low1, before, total0, total1, held1):
+def third_second(held0, square1, before, *rest):
+    w_high0, w_low0, w_high1, w_low1 = [rest[k * PAIRS : (k + 1) * PAIRS] for k in range(4)]
+    total0, total1, held1 = rest[4 * PAIRS :]
     lift(square1, held1)
     total0[...] = before[...]
     total1[...] = jnp.zeros_like(total1)
@@ -207,29 +221,43 @@
     add_products(total1, held1, 1, w_high1, w_low1)
 
 
-def third_outer(halo, w_high0, w_low0, before, total0, held):
-    total0[...] = before[...]
-    lift_halo(halo, held, WIDE - HALO)
-    add_products(total0, held, 0, w_high0, w_low0)
-
-
-def finish(codes, halo, square0, square1, w_high1, w_low1, total0, before1, out, total1, held):
+def finish(codes, halo0, halo1, square0, square1, before0, before1, *rest):
+    w_high0, w_low0, w_high1, w_low1 = [rest[k * PAIRS : (k + 1) * PAIRS] for k in range(4)]
+    out, total, held0, held1, ready, sems = rest[4 * PAIRS :]
     core = lax.rem(lax.axis_index("row"), 2)
-    lift_halo(halo, held, 0)
-    total1[...] = before1[...]
-    add_products(total1, held, 2, w_high1, w_low1)
-    for chunk, (square, total) in enumerate(((square0, total0), (square1, total1))):
+
+    def write(chunk, square):
         for i in range(PAIRS):
             value = 3.0 * square[i, 6 * COLS : 6 * COLS + VIEW] - 2.0 * total[i]
             for q in range(2):
-                r = flipped(core, chunk * HALF + 2 * i + q, 2 * HALF - 1)
-                rest = unused_slots(codes[r, 0])
+                v = 2 * i + q
+                spot = flipped(core, v, HALF - 1)
+                rest = unused_slots(code_of(codes, core, chunk * HALF + v))
                 for s in range(SLOTS):
-                    out[r, flipped(core, s, SLOTS - 1)] = value[(s + q) * COLS : (s + q + 1) * COLS, q * B : (q + 1) * B]
+                    tile = value[(s + q) * COLS : (s + q + 1) * COLS, q * B : (q + 1) * B]
+                    ready[chunk, spot, flipped(core, s, SLOTS - 1)] = tile
                 for t in range(SLOTS - ONES):
-                    out[r, flipped(core, slot_of(rest, t), SLOTS - 1)] = jnp.zeros((COLS, B), F32)
-
-
+                    place = flipped(core, slot_of(rest, t), SLOTS - 1)
+                    ready[chunk, spot, place] = jnp.zeros((COLS, B), F32)
+        rows = pl.ds(flipped(core, chunk * HALF, HALF), HALF)
+        copy = pltpu.make_async_copy(ready.at[chunk], out.at[rows], sems.at[chunk])
+        copy.start()
+        return copy
+
+    lift_halo(halo0, held0, WIDE - HALO)
+    total[...] = before0[...]
+    add_products(total, held0, 0, w_high0, w_low0)
+    first = write(0, square0)
+    lift_halo(halo1, held1, 0)
+    total[...] = before1[...]
+    add_products(total, held1, 2, w_high1, w_low1)
+    second = write(1, square1)
+    first.wait()
+    second.wait()
+
+
+ANY = pl.BlockSpec(memory_space=pl.ANY)
+HBM = pl.BlockSpec(memory_space=pltpu.HBM)
 VMEM = pl.BlockSpec(memory_space=pltpu.VMEM)
 PARAMS = pltpu.CompilerParams(vmem_limit_bytes=16 * 1024 * 1024)
 
@@ -265,11 +293,19 @@
     packed, dense0, dense1, codes = pl.pallas_call(
         prepare,
         out_shape=(shape(4, 2 * CHUNK, COLS, B), dense_shape, dense_shape, shape(2 * HALF, B, dtype=jnp.int32)),
-        in_specs=[VMEM, VMEM],
+        in_specs=[HBM, HBM],
         out_specs=(VMEM,) * 4,
+        scratch_shapes=[
+            pltpu.VMEM(pattern.shape, jnp.int32),
+            pltpu.VMEM(density.shape, F32),
+            pltpu.SemaphoreType.DMA((2,)),
+        ],
         compiler_params=PARAMS,
         name="prepare",
-    )(pattern, density)
+    )(
+        pltpu.with_memory_space_constraint(pattern, pltpu.HBM),
+        pltpu.with_memory_space_constraint(density, pltpu.HBM),
+    )
 
     quads = []
     for z in range(16):
@@ -282,21 +318,21 @@
         part = near[:, chunk * CHUNK : (chunk + 1) * CHUNK]
         far.append([send(part, second_way(step)) for step in (1, -1, 2)])
     halo_z = send(dense0, next_chip)
-    weights = shape(PAIRS, DEPTH, 2 * B, dtype=BF16)
+    weights = (shape(DEPTH, 2 * B, dtype=BF16),) * (2 * PAIRS)
 
     def squared(chunk, *sides):
         return pl.pallas_call(
             functools.partial(square_kernel, chunk),
-            out_shape=(shape(PAIRS, WIDE, 2 * B), shape(PAIRS, HALO, 2 * B), weights, weights),
+            out_shape=(shape(PAIRS, WIDE, 2 * B), shape(PAIRS, HALO, 2 * B), *weights),
             in_specs=[VMEM] * 8,
-            out_specs=(VMEM,) * 4,
+            out_specs=(VMEM,) * (2 + 2 * PAIRS),
             scratch_shapes=[pltpu.VMEM((CHUNK, B, B), F32), pltpu.VMEM((3 * PAIRS, 2 * VIEW, 2 * B), BF16)],
             compiler_params=PARAMS,
             cost_estimate=cost(21),
             name=f"square{chunk}",
         )(codes, near, *far[chunk], *sides)
 
-    square0, edge0, w_high0, w_low0 = squared(0, halo_z, dense0, dense1)
+    square0, edge0, *w0 = squared(0, halo_z, dense0, dense1)
     square_z = send(edge0, next_chip)
     totals = shape(PAIRS, VIEW, 2 * B)
     held_shape = (2, PAIRS, WIDE, 2 * B)
@@ -304,48 +340,43 @@
     total0, held0 = pl.pallas_call(
         third_inner,
         out_shape=(totals, shape(*held_shape, dtype=BF16)),
-        in_specs=[VMEM] * 3,
+        in_specs=[VMEM] * (1 + 2 * PAIRS),
         out_specs=(VMEM, VMEM),
         compiler_params=PARAMS,
         cost_estimate=cost(9),
         name="third_inner",
-    )(square0, w_high0, w_low0)
+    )(square0, *w0)
     dense1_later, far[1][2] = lax.optimization_barrier((dense1, far[1][2]))
     halo_c = send(dense1_later, other_core)
     halo_c, held0 = lax.optimization_barrier((halo_c, held0))
-    square1, edge1, w_high1, w_low1 = squared(1, dense0, dense1, halo_c)
+    square1, edge1, *w1 = squared(1, dense0, dense1, halo_c)
     square_c = send(edge1, other_core)
     total0, total1 = pl.pallas_call(
         third_second,
         out_shape=(totals, totals),
-        in_specs=[VMEM] * 7,
+        in_specs=[VMEM] * (3 + 4 * PAIRS),
         out_specs=(VMEM, VMEM),
         scratch_shapes=[held],
         compiler_params=PARAMS,
         cost_estimate=cost(21),
         name="third_second",
-    )(held0, square1, w_high0, w_low0, w_high1, w_low1, total0)
-    square_z, total0 = lax.optimization_barrier((square_z, total0))
-    total0 = pl.pallas_call(
-        third_outer,
-        out_shape=totals,
-        in_specs=[VMEM] * 4,
-        out_specs=VMEM,
-        scratch_shapes=[held],
-        compiler_params=PARAMS,
-        cost_estimate=cost(6),
-        name="third_outer",
-    )(square_z, w_high0, w_low0, total0)
+    )(held0, square1, total0, *w0, *w1)
     return pl.pallas_call(
         finish,
         out_shape=shape(2 * HALF, SLOTS, COLS, B),
-        in_specs=[VMEM] * 8,
-        out_specs=VMEM,
-        scratch_shapes=[pltpu.VMEM((PAIRS, VIEW, 2 * B), F32), held],
+        in_specs=[VMEM] * (7 + 4 * PAIRS),
+        out_specs=ANY,
+        scratch_shapes=[
+            pltpu.VMEM((PAIRS, VIEW, 2 * B), F32),
+            held,
+            held,
+            pltpu.VMEM((2, HALF, SLOTS, COLS, B), F32),
+            pltpu.SemaphoreType.DMA((2,)),
+        ],
         compiler_params=PARAMS,
-        cost_estimate=cost(6),
+        cost_estimate=cost(12),
         name="finish",
-    )(codes, square_c, square0, square1, w_high1, w_low1, total0, total1)
+    )(codes, square_z, square_c, square0, square1, total0, total1, *w0, *w1)
 
 
 def solution(mesh):

time: 70.4 us -> 69.2 us (0.983)
  local copies, waits for them, and re-layouts: 1.87 us -> 0.09 us
    unnamed x4 -> x0, local copies, waits for them, and re-layouts: 1.78 us -> none
    pallas_call x1, Pallas kernels: 0.45 us -> 1.38 us  [shards(): pl.pallas_call(prepare, out_shape=(shape(4, 2 * CHUNK, COLS, B), dense_sh...]
  transfers between devices with their start and end apart: 10 -> 10, of which waited for: 0 -> 0; matrix products, arithmetic and copies ran while one was open for 0% -> 0% of each run, Pallas kernels for 11% -> 10%
where the time goes in v4:
time: 69.2 us; the launch traced here: 68.7 us
  starting transfers between devices  41.8 us (60%)
  blocking collectives  16.3 us (24%)
  Pallas kernels  10.3 us (15%)
    ppermute x10, starting transfers between devices, send(): lax.ppermute(value, AXES, [(number(*spot), number(*move(*spot))) for spot...  41.8 us
    all_to_all x1, blocking collectives, shards(): near = lax.all_to_all(packed, AXES, 0, 0, axis_index_groups=quads)  16.3 us
    pallas_call x2, Pallas kernels, squared(): pl.pallas_call(functools.partial(square_kernel, chunk), out_shape=(shape(...  4.96 us
    pallas_call x1, Pallas kernels, shards(): pl.pallas_call(finish, out_shape=shape(2 * HALF, SLOTS, COLS, B), in_spec...  1.91 us
  transfers between devices with their start and end apart: 10, of which 0 were waited for; matrix products, arithmetic and copies ran while one was open for 0% of the time, Pallas kernels for 10%

profile of v4, /device:TPU:1, one launch (start us, length us, event | category | flops | bytes accessed | tf_op | source)
XLA Modules:
  0.0 68.7 jit_solution(4696308262487186615)
XLA Ops:
  0.0 1.4 %prepare.1 = (f32[4,84,8,128]{3,2,1,0:T(8,128)S(1)}, f32[6,13,8,128]{3,2,1,0:T(8,128)S(1)}, f32[6,13,8,128]{3,2,1,0:T(8,128)S(1)}, s32[12,128]{1,0:T(8,128)S(1)}) custom-call(s32[12,13]{1,0:T(8,128)} %pattern_far.1, f32[12,13,8,128]{3,2,1,0:T(8,128)} %density_far.1), custom_call_target="tpu_custom_call" | custom-call | tf_op jit(solution)/shard_map/prepare/pallas_call | solution.py:293
  1.4 16.3 %all_to_all.5.near = f32[4,84,8,128]{3,2,1,0:T(8,128)S(1)} all-to-all(f32[4,84,8,128]{3,2,1,0:T(8,128)S(1)} %get-tuple-element.34), channel_id=1, replica_groups={{0,1,2,3},{16,20,24,28},{4,5,6,7},{17,21,25,29},{8,9,10,11},{18,22,26,3..., dimensions={0} | all-to-all | bytes 2752512 | tf_op jit(solution)/shard_map/all_to_all | solution.py:315
  17.7 0.1 fusion
  17.8 4.7 %collective-permute-start.7 = (f32[4,42,8,128]{3,2,1,0:T(8,128)S(1)}, f32[4,42,8,128]{3,2,1,0:T(8,128)S(1)}, u32[]{:S(2)}, u32[]{:S(2)}) collective-permute-start(f32[4,42,8,128]{3,2,1,0:T(8,128)S(1)} %get-tuple-element.61), channel_id=1, source_target_pairs={{0,8},{1,9},{2,10},{3,11},{4,12},{5,13},{6,14},{7,15},{8,0},{9,1},... | collective-permute-start | bytes 2064392 | tf_op jit(solution)/shard_map/ppermute | solution.py:281
  22.5 2.1 %collective-permute-start.2 = (f32[4,42,8,128]{3,2,1,0:T(8,128)S(1)}, f32[4,42,8,128]{3,2,1,0:T(8,128)S(1)}, u32[]{:S(2)}, u32[]{:S(2)}) collective-permute-start(f32[4,42,8,128]{3,2,1,0:T(8,128)S(1)} %get-tuple-element.62), channel_id=1, source_target_pairs={{0,8},{1,9},{2,10},{3,11},{4,12},{5,13},{6,14},{7,15},{8,0},{9,1},... | collective-permute-start | bytes 2064392 | tf_op jit(solution)/shard_map/ppermute | solution.py:281
  24.6 5.9 %collective-permute-start.3 = (f32[6,13,8,128]{3,2,1,0:T(8,128)S(1)}, f32[6,13,8,128]{3,2,1,0:T(8,128)S(1)}, u32[]{:S(2)}, u32[]{:S(2)}) collective-permute-start(f32[6,13,8,128]{3,2,1,0:T(8,128)S(1)} %get-tuple-element.35.middle.before), channel_id=1, source_target_pairs={{0,496},{1,497},{2,498},{3,499},{4,500},{5,501},{6,502},{7,503},{8... | collective-permute-start | bytes 958472 | tf_op jit(solution)/shard_map/ppermute | solution.py:281
  30.5 2.8 %collective-permute-start.1 = (f32[4,42,8,128]{3,2,1,0:T(8,128)S(1)}, f32[4,42,8,128]{3,2,1,0:T(8,128)S(1)}, u32[]{:S(2)}, u32[]{:S(2)}) collective-permute-start(f32[4,42,8,128]{3,2,1,0:T(8,128)S(1)} %get-tuple-element.62), channel_id=1, source_target_pairs={{0,12},{1,13},{2,14},{3,15},{4,0},{5,1},{6,2},{7,3},{8,4},{9,5},{1... | collective-permute-start | bytes 2064392 | tf_op jit(solution)/shard_map/ppermute | solution.py:281
  33.3 2.5 %collective-permute-start = (f32[4,42,8,128]{3,2,1,0:T(8,128)S(1)}, f32[4,42,8,128]{3,2,1,0:T(8,128)S(1)}, u32[]{:S(2)}, u32[]{:S(2)}) collective-permute-start(f32[4,42,8,128]{3,2,1,0:T(8,128)S(1)} %get-tuple-element.62), channel_id=1, source_target_pairs={{0,4},{1,5},{2,6},{3,7},{4,8},{5,9},{6,10},{7,11},{8,12},{9,13},{1... | collective-permute-start | bytes 2064392 | tf_op jit(solution)/shard_map/ppermute | solution.py:281
  35.8 0.0 collective-permute-done.3.before
  35.8 4.0 %collective-permute-start.6 = (f32[4,42,8,128]{3,2,1,0:T(8,128)S(1)}, f32[4,42,8,128]{3,2,1,0:T(8,128)S(1)}, u32[]{:S(2)}, u32[]{:S(2)}) collective-permute-start(f32[4,42,8,128]{3,2,1,0:T(8,128)S(1)} %get-tuple-element.61), channel_id=1, source_target_pairs={{0,12},{1,13},{2,14},{3,15},{4,0},{5,1},{6,2},{7,3},{8,4},{9,5},{1... | collective-permute-start | bytes 2064392 | tf_op jit(solution)/shard_map/ppermute | solution.py:281
  39.9 0.0 collective-permute-done.7.far_o
  39.9 1.9 %collective-permute-start.5 = (f32[4,42,8,128]{3,2,1,0:T(8,128)S(1)}, f32[4,42,8,128]{3,2,1,0:T(8,128)S(1)}, u32[]{:S(2)}, u32[]{:S(2)}) collective-permute-start(f32[4,42,8,128]{3,2,1,0:T(8,128)S(1)} %get-tuple-element.61), channel_id=1, source_target_pairs={{0,4},{1,5},{2,6},{3,7},{4,8},{5,9},{6,10},{7,11},{8,12},{9,13},{1... | collective-permute-start | bytes 2064392 | tf_op jit(solution)/shard_map/ppermute | solution.py:281
  41.8 0.0 collective-permute-done.2.far_o
  41.8 8.6 %collective-permute-start.8 = (f32[6,13,8,128]{3,2,1,0:T(8,128)S(1)}, f32[6,13,8,128]{3,2,1,0:T(8,128)S(1)}, u32[]{:S(2)}, u32[]{:S(2)}) collective-permute-start(f32[6,13,8,128]{3,2,1,0:T(8,128)S(1)} %get-tuple-element.39.after.middle), channel_id=1, source_target_pairs={{0,16},{1,17},{2,18},{3,19},{4,20},{5,21},{6,22},{7,23},{8,24},{9,... | collective-permute-start | bytes 958472 | tf_op jit(solution)/shard_map/ppermute | solution.py:281
  50.4 0.0 collective-permute-done.1.far_p
  50.4 0.0 collective-permute-done.far_m
  50.4 2.5 %square0.1 = (f32[3,208,256]{2,1,0:T(8,128)S(1)}, f32[3,144,256]{2,1,0:T(8,128)S(1)}, bf16[1792,256]{1,0:T(8,128)(2,1)S(1)}, bf16[1792,256]{1,0:T(8,128)(2,1)S(1...) custom-call(s32[12,128]{1,0:T(8,128)S(1)} %get-tuple-element.33.code, ...), custom_call_target="tpu_custom_call" | custom-call | flops 924844032 | bytes 4000000 | tf_op jit(solution)/shard_map/square0/pallas_call | solution.py:324
  52.9 2.2 %collective-permute-start.4 = (f32[3,144,256]{2,1,0:T(8,128)S(1)}, f32[3,144,256]{2,1,0:T(8,128)S(1)}, u32[]{:S(2)}, u32[]{:S(2)}) collective-permute-start(f32[3,144,256]{2,1,0:T(8,128)S(1)} %get-tuple-element.37), channel_id=1, source_target_pairs={{0,496},{1,497},{2,498},{3,499},{4,500},{5,501},{6,502},{7,503},{8... | collective-permute-start | bytes 1327112 | tf_op jit(solution)/shard_map/ppermute | solution.py:281
  55.1 0.7 %third_inner.1 = (f32[3,112,256]{2,1,0:T(8,128)S(1)}, bf16[2,3,208,256]{3,2,1,0:T(8,128)(2,1)S(1)}) custom-call(f32[3,208,256]{2,1,0:T(8,128)S(1)} %get-tuple-element.40.square0, bf16[1792,256]{1,0:T(8,128)(2,1)S(1)} %get-tuple-element.41.rest_0_, bf16[1792,256]{1,0:T(8,128)(2,1)S(1)} %get-tuple-element.42.rest_1_, ...), custom_call_target="tpu_custom_call" | custom-call | flops 396361728 | bytes 4000000 | tf_op jit(solution)/shard_map/third_inner/pallas_call | solution.py:340
  55.8 0.0 collective-permute-done.8.after
  55.8 0.0 collective-permute-done.6.far_p
  55.8 0.0 collective-permute-done.5.far_m
  55.8 2.5 %square1.1 = (f32[3,208,256]{2,1,0:T(8,128)S(1)}, f32[3,144,256]{2,1,0:T(8,128)S(1)}, bf16[1792,256]{1,0:T(8,128)(2,1)S(1)}, bf16[1792,256]{1,0:T(8,128)(2,1)S(1...) custom-call(s32[12,128]{1,0:T(8,128)S(1)} %get-tuple-element.33.code, ...), custom_call_target="tpu_custom_call" | custom-call | flops 924844032 | bytes 4000000 | tf_op jit(solution)/shard_map/square1/pallas_call | solution.py:324
  58.3 7.1 %collective-permute-start.9 = (f32[3,144,256]{2,1,0:T(8,128)S(1)}, f32[3,144,256]{2,1,0:T(8,128)S(1)}, u32[]{:S(2)}, u32[]{:S(2)}) collective-permute-start(f32[3,144,256]{2,1,0:T(8,128)S(1)} %get-tuple-element.49), channel_id=1, source_target_pairs={{0,16},{1,17},{2,18},{3,19},{4,20},{5,21},{6,22},{7,23},{8,24},{9,... | collective-permute-start | bytes 1327112 | tf_op jit(solution)/shard_map/ppermute | solution.py:281
  65.4 1.3 %third_second.1 = (f32[3,112,256]{2,1,0:T(8,128)S(1)}, f32[3,112,256]{2,1,0:T(8,128)S(1)}) custom-call(bf16[2,3,208,256]{3,2,1,0:T(8,128)(2,1)S(1)} %get-tuple-element.51.held0, f32[3,208,256]{2,1,0:T(8,128)S(1)} %get-tuple-element.50.square1, f32[3,112,256]{2,1,0:T(8,128)S(1)} %get-tuple-element.52.before, bf16[1792,256]{1,0:T(8,128)(2,1)S(1)} %get-tuple-element.41.rest_0_, ...), custom_call_target="tpu_custom_call" | custom-call | flops 924844032 | bytes 4000000 | tf_op jit(solution)/shard_map/third_second/pallas_call | solution.py:354
  66.8 0.0 collective-permute-done.4.halo0
  66.8 0.0 collective-permute-done.9.halo1
  66.8 1.9 %finish.1 = f32[12,13,8,128]{3,2,1,0:T(8,128)} custom-call(s32[12,128]{1,0:T(8,128)S(1)} %get-tuple-element.33.codes, f32[3,144,256]{2,1,0:T(8,128)S(1)} %collective-permute-done.4.halo0, f32[3,144,256]{2,1,0:T(8,128)S(1)} %collective-permute-done.9.halo1, f32[3,208,256]{2,1,0:T(8,128)S(1)} %get-tuple-element.40.square0, ...), custom_call_target="tpu_custom_call" | custom-call | flops 528482304 | bytes 4000000 | tf_op jit(solution)/shard_map/finish/pallas_call | solution.py:364
Async XLA Ops:
  17.8 22.1 %collective-permute-start.7 = (f32[4,42,8,128]{3,2,1,0:T(8,128)S(1)}, f32[4,42,8,128]{3,2,1,0:T(8,128)S(1)}, u32[]{:S(2)}, u32[]{:S(2)}) collective-permute-start(f32[4,42,8,128]{3,2,1,0:T(8,128)S(1)} %get-tuple-element.61), channel_id=1, source_target_pairs={{0,8},{1,9},{2,10},{3,11},{4,12},{5,13},{6,14},{7,15},{8,0},{9,1},... | collective-permute-start | bytes 2064392 | tf_op jit(solution)/shard_map/ppermute | solution.py:281
  22.5 19.3 %collective-permute-start.2 = (f32[4,42,8,128]{3,2,1,0:T(8,128)S(1)}, f32[4,42,8,128]{3,2,1,0:T(8,128)S(1)}, u32[]{:S(2)}, u32[]{:S(2)}) collective-permute-start(f32[4,42,8,128]{3,2,1,0:T(8,128)S(1)} %get-tuple-element.62), channel_id=1, source_target_pairs={{0,8},{1,9},{2,10},{3,11},{4,12},{5,13},{6,14},{7,15},{8,0},{9,1},... | collective-permute-start | bytes 2064392 | tf_op jit(solution)/shard_map/ppermute | solution.py:281
  24.6 11.2 %collective-permute-start.3 = (f32[6,13,8,128]{3,2,1,0:T(8,128)S(1)}, f32[6,13,8,128]{3,2,1,0:T(8,128)S(1)}, u32[]{:S(2)}, u32[]{:S(2)}) collective-permute-start(f32[6,13,8,128]{3,2,1,0:T(8,128)S(1)} %get-tuple-element.35.middle.before), channel_id=1, source_target_pairs={{0,496},{1,497},{2,498},{3,499},{4,500},{5,501},{6,502},{7,503},{8... | collective-permute-start | bytes 958472 | tf_op jit(solution)/shard_map/ppermute | solution.py:281
  30.5 19.8 %collective-permute-start.1 = (f32[4,42,8,128]{3,2,1,0:T(8,128)S(1)}, f32[4,42,8,128]{3,2,1,0:T(8,128)S(1)}, u32[]{:S(2)}, u32[]{:S(2)}) collective-permute-start(f32[4,42,8,128]{3,2,1,0:T(8,128)S(1)} %get-tuple-element.62), channel_id=1, source_target_pairs={{0,12},{1,13},{2,14},{3,15},{4,0},{5,1},{6,2},{7,3},{8,4},{9,5},{1... | collective-permute-start | bytes 2064392 | tf_op jit(solution)/shard_map/ppermute | solution.py:281
  33.3 17.1 %collective-permute-start = (f32[4,42,8,128]{3,2,1,0:T(8,128)S(1)}, f32[4,42,8,128]{3,2,1,0:T(8,128)S(1)}, u32[]{:S(2)}, u32[]{:S(2)}) collective-permute-start(f32[4,42,8,128]{3,2,1,0:T(8,128)S(1)} %get-tuple-element.62), channel_id=1, source_target_pairs={{0,4},{1,5},{2,6},{3,7},{4,8},{5,9},{6,10},{7,11},{8,12},{9,13},{1... | collective-permute-start | bytes 2064392 | tf_op jit(solution)/shard_map/ppermute | solution.py:281
  35.8 20.0 %collective-permute-start.6 = (f32[4,42,8,128]{3,2,1,0:T(8,128)S(1)}, f32[4,42,8,128]{3,2,1,0:T(8,128)S(1)}, u32[]{:S(2)}, u32[]{:S(2)}) collective-permute-start(f32[4,42,8,128]{3,2,1,0:T(8,128)S(1)} %get-tuple-element.61), channel_id=1, source_target_pairs={{0,12},{1,13},{2,14},{3,15},{4,0},{5,1},{6,2},{7,3},{8,4},{9,5},{1... | collective-permute-start | bytes 2064392 | tf_op jit(solution)/shard_map/ppermute | solution.py:281
  39.9 16.0 %collective-permute-start.5 = (f32[4,42,8,128]{3,2,1,0:T(8,128)S(1)}, f32[4,42,8,128]{3,2,1,0:T(8,128)S(1)}, u32[]{:S(2)}, u32[]{:S(2)}) collective-permute-start(f32[4,42,8,128]{3,2,1,0:T(8,128)S(1)} %get-tuple-element.61), channel_id=1, source_target_pairs={{0,4},{1,5},{2,6},{3,7},{4,8},{5,9},{6,10},{7,11},{8,12},{9,13},{1... | collective-permute-start | bytes 2064392 | tf_op jit(solution)/shard_map/ppermute | solution.py:281
  41.8 14.0 %collective-permute-start.8 = (f32[6,13,8,128]{3,2,1,0:T(8,128)S(1)}, f32[6,13,8,128]{3,2,1,0:T(8,128)S(1)}, u32[]{:S(2)}, u32[]{:S(2)}) collective-permute-start(f32[6,13,8,128]{3,2,1,0:T(8,128)S(1)} %get-tuple-element.39.after.middle), channel_id=1, source_target_pairs={{0,16},{1,17},{2,18},{3,19},{4,20},{5,21},{6,22},{7,23},{8,24},{9,... | collective-permute-start | bytes 958472 | tf_op jit(solution)/shard_map/ppermute | solution.py:281
  52.9 13.9 %collective-permute-start.4 = (f32[3,144,256]{2,1,0:T(8,128)S(1)}, f32[3,144,256]{2,1,0:T(8,128)S(1)}, u32[]{:S(2)}, u32[]{:S(2)}) collective-permute-start(f32[3,144,256]{2,1,0:T(8,128)S(1)} %get-tuple-element.37), channel_id=1, source_target_pairs={{0,496},{1,497},{2,498},{3,499},{4,500},{5,501},{6,502},{7,503},{8... | collective-permute-start | bytes 1327112 | tf_op jit(solution)/shard_map/ppermute | solution.py:281
  58.3 8.5 %collective-permute-start.9 = (f32[3,144,256]{2,1,0:T(8,128)S(1)}, f32[3,144,256]{2,1,0:T(8,128)S(1)}, u32[]{:S(2)}, u32[]{:S(2)}) collective-permute-start(f32[3,144,256]{2,1,0:T(8,128)S(1)} %get-tuple-element.49), channel_id=1, source_target_pairs={{0,16},{1,17},{2,18},{3,19},{4,20},{5,21},{6,22},{7,23},{8,24},{9,... | collective-permute-start | bytes 1327112 | tf_op jit(solution)/shard_map/ppermute | solution.py:281

commit v5 on v4

--- a/solution.py
+++ b/solution.py
@@ -16,7 +16,7 @@
 PAIRS = HALF // 2
 VIEW = 14 * COLS
 WIDE = 26 * COLS
-HALO = 18 * COLS
+HALO = 48 * COLS
 DEPTH = 14 * B
 F32 = jnp.float32
 BF16 = jnp.bfloat16
@@ -145,6 +145,11 @@
             w_low[rows, lanes] = low
 
 
+def edge_of(chunk, i):
+    lengths = [(18 - 2 * k) * COLS if chunk == 0 else (14 + 2 * k) * COLS for k in range(PAIRS)]
+    return lengths[i], sum(lengths[:i])
+
+
 def squares(chunk, i, sides, w_high, w_low, square, halo):
     square[i] = jnp.zeros((WIDE, 2 * B), F32)
     for m in range(7):
@@ -152,10 +157,9 @@
         whole = jnp.dot(sides[i + m], w_high[depth], preferred_element_type=F32)
         small = jnp.dot(sides[i + m, :VIEW], w_low[depth], preferred_element_type=F32)
         square[i, 2 * COLS * m : 2 * COLS * m + VIEW] += whole[:VIEW] + whole[VIEW:] + small
-    if chunk == 0:
-        halo[i] = square[i, :HALO]
-    else:
-        halo[i] = square[i, WIDE - HALO :]
+    length, start = edge_of(chunk, i)
+    first = 0 if chunk == 0 else WIDE - length
+    halo[start : start + length] = square[i, first : first + length]
 
 
 def square_kernel(chunk, codes, near, far_m, far_p, far_o, before, middle, after, square, halo, *rest):
@@ -174,14 +178,15 @@
         held[0, i], held[1, i] = split(ref[i])
 
 
-def lift_halo(ref, held, first):
+def lift_halo(ref, held, chunk):
     for i in range(PAIRS):
-        source = ref[PAIRS - 1 - i]
-        turned = jnp.concatenate(
-            [source[(HALO // COLS - 1 - j) * COLS : (HALO // COLS - j) * COLS] for j in range(HALO // COLS)], axis=0
-        )
+        length, start = edge_of(chunk, PAIRS - 1 - i)
+        count = length // COLS
+        source = ref[start : start + length]
+        turned = jnp.concatenate([source[(count - 1 - j) * COLS : (count - j) * COLS] for j in range(count)], axis=0)
         turned = jnp.concatenate([turned[:, B:], turned[:, :B]], axis=1)
-        held[0, i, first : first + HALO], held[1, i, first : first + HALO] = split(turned)
+        first = WIDE - length if chunk == 0 else 0
+        held[0, i, first : first + length], held[1, i, first : first + length] = split(turned)
 
 
 def add_products(total, held, part, w_high, w_low):
@@ -244,11 +249,11 @@
         copy.start()
         return copy
 
-    lift_halo(halo0, held0, WIDE - HALO)
+    lift_halo(halo0, held0, 0)
     total[...] = before0[...]
     add_products(total, held0, 0, w_high0, w_low0)
     first = write(0, square0)
-    lift_halo(halo1, held1, 0)
+    lift_halo(halo1, held1, 1)
     total[...] = before1[...]
     add_products(total, held1, 2, w_high1, w_low1)
     second = write(1, square1)
@@ -323,7 +328,7 @@
     def squared(chunk, *sides):
         return pl.pallas_call(
             functools.partial(square_kernel, chunk),
-            out_shape=(shape(PAIRS, WIDE, 2 * B), shape(PAIRS, HALO, 2 * B), *weights),
+            out_shape=(shape(PAIRS, WIDE, 2 * B), shape(HALO, 2 * B), *weights),
             in_specs=[VMEM] * 8,
             out_specs=(VMEM,) * (2 + 2 * PAIRS),
             scratch_shapes=[pltpu.VMEM((CHUNK, B, B), F32), pltpu.VMEM((3 * PAIRS, 2 * VIEW, 2 * B), BF16)],

time: 69.2 us -> 69.2 us (level)
  no operation moved by 1% of the time
where the time goes in v5:
time: 69.2 us; the launch traced here: 68.7 us
  starting transfers between devices  41.8 us (60%)
  blocking collectives  16.3 us (24%)
  Pallas kernels  10.3 us (15%)
    ppermute x10, starting transfers between devices, send(): lax.ppermute(value, AXES, [(number(*spot), number(*move(*spot))) for spot...  41.8 us
    all_to_all x1, blocking collectives, shards(): near = lax.all_to_all(packed, AXES, 0, 0, axis_index_groups=quads)  16.3 us
    pallas_call x2, Pallas kernels, squared(): pl.pallas_call(functools.partial(square_kernel, chunk), out_shape=(shape(...  4.96 us
    pallas_call x1, Pallas kernels, shards(): pl.pallas_call(finish, out_shape=shape(2 * HALF, SLOTS, COLS, B), in_spec...  1.92 us
  transfers between devices with their start and end apart: 10, of which 0 were waited for; matrix products, arithmetic and copies ran while one was open for 0% of the time, Pallas kernels for 10%

profile of v5, /device:TPU:1, one launch (start us, length us, event | category | flops | bytes accessed | tf_op | source)
XLA Modules:
  0.0 68.7 jit_solution(4425759884395950794)
XLA Ops:
  0.0 1.4 %prepare.1 = (f32[4,84,8,128]{3,2,1,0:T(8,128)S(1)}, f32[6,13,8,128]{3,2,1,0:T(8,128)S(1)}, f32[6,13,8,128]{3,2,1,0:T(8,128)S(1)}, s32[12,128]{1,0:T(8,128)S(1)}) custom-call(s32[12,13]{1,0:T(8,128)} %pattern_far.1, f32[12,13,8,128]{3,2,1,0:T(8,128)} %density_far.1), custom_call_target="tpu_custom_call" | custom-call | tf_op jit(solution)/shard_map/prepare/pallas_call | solution.py:298
  1.4 16.3 %all_to_all.5.near = f32[4,84,8,128]{3,2,1,0:T(8,128)S(1)} all-to-all(f32[4,84,8,128]{3,2,1,0:T(8,128)S(1)} %get-tuple-element.34), channel_id=1, replica_groups={{0,1,2,3},{16,20,24,28},{4,5,6,7},{17,21,25,29},{8,9,10,11},{18,22,26,3..., dimensions={0} | all-to-all | bytes 2752512 | tf_op jit(solution)/shard_map/all_to_all | solution.py:320
  17.7 0.1 fusion
  17.8 4.7 %collective-permute-start.7 = (f32[4,42,8,128]{3,2,1,0:T(8,128)S(1)}, f32[4,42,8,128]{3,2,1,0:T(8,128)S(1)}, u32[]{:S(2)}, u32[]{:S(2)}) collective-permute-start(f32[4,42,8,128]{3,2,1,0:T(8,128)S(1)} %get-tuple-element.61), channel_id=1, source_target_pairs={{0,8},{1,9},{2,10},{3,11},{4,12},{5,13},{6,14},{7,15},{8,0},{9,1},... | collective-permute-start | bytes 2064392 | tf_op jit(solution)/shard_map/ppermute | solution.py:286
  22.5 2.1 %collective-permute-start.2 = (f32[4,42,8,128]{3,2,1,0:T(8,128)S(1)}, f32[4,42,8,128]{3,2,1,0:T(8,128)S(1)}, u32[]{:S(2)}, u32[]{:S(2)}) collective-permute-start(f32[4,42,8,128]{3,2,1,0:T(8,128)S(1)} %get-tuple-element.62), channel_id=1, source_target_pairs={{0,8},{1,9},{2,10},{3,11},{4,12},{5,13},{6,14},{7,15},{8,0},{9,1},... | collective-permute-start | bytes 2064392 | tf_op jit(solution)/shard_map/ppermute | solution.py:286
  24.6 5.9 %collective-permute-start.3 = (f32[6,13,8,128]{3,2,1,0:T(8,128)S(1)}, f32[6,13,8,128]{3,2,1,0:T(8,128)S(1)}, u32[]{:S(2)}, u32[]{:S(2)}) collective-permute-start(f32[6,13,8,128]{3,2,1,0:T(8,128)S(1)} %get-tuple-element.35.middle.before), channel_id=1, source_target_pairs={{0,496},{1,497},{2,498},{3,499},{4,500},{5,501},{6,502},{7,503},{8... | collective-permute-start | bytes 958472 | tf_op jit(solution)/shard_map/ppermute | solution.py:286
  30.5 2.8 %collective-permute-start.1 = (f32[4,42,8,128]{3,2,1,0:T(8,128)S(1)}, f32[4,42,8,128]{3,2,1,0:T(8,128)S(1)}, u32[]{:S(2)}, u32[]{:S(2)}) collective-permute-start(f32[4,42,8,128]{3,2,1,0:T(8,128)S(1)} %get-tuple-element.62), channel_id=1, source_target_pairs={{0,12},{1,13},{2,14},{3,15},{4,0},{5,1},{6,2},{7,3},{8,4},{9,5},{1... | collective-permute-start | bytes 2064392 | tf_op jit(solution)/shard_map/ppermute | solution.py:286
  33.3 2.5 %collective-permute-start = (f32[4,42,8,128]{3,2,1,0:T(8,128)S(1)}, f32[4,42,8,128]{3,2,1,0:T(8,128)S(1)}, u32[]{:S(2)}, u32[]{:S(2)}) collective-permute-start(f32[4,42,8,128]{3,2,1,0:T(8,128)S(1)} %get-tuple-element.62), channel_id=1, source_target_pairs={{0,4},{1,5},{2,6},{3,7},{4,8},{5,9},{6,10},{7,11},{8,12},{9,13},{1... | collective-permute-start | bytes 2064392 | tf_op jit(solution)/shard_map/ppermute | solution.py:286
  35.8 0.0 collective-permute-done.3.before
  35.8 4.0 %collective-permute-start.6 = (f32[4,42,8,128]{3,2,1,0:T(8,128)S(1)}, f32[4,42,8,128]{3,2,1,0:T(8,128)S(1)}, u32[]{:S(2)}, u32[]{:S(2)}) collective-permute-start(f32[4,42,8,128]{3,2,1,0:T(8,128)S(1)} %get-tuple-element.61), channel_id=1, source_target_pairs={{0,12},{1,13},{2,14},{3,15},{4,0},{5,1},{6,2},{7,3},{8,4},{9,5},{1... | collective-permute-start | bytes 2064392 | tf_op jit(solution)/shard_map/ppermute | solution.py:286
  39.9 0.0 collective-permute-done.7.far_o
  39.9 1.9 %collective-permute-start.5 = (f32[4,42,8,128]{3,2,1,0:T(8,128)S(1)}, f32[4,42,8,128]{3,2,1,0:T(8,128)S(1)}, u32[]{:S(2)}, u32[]{:S(2)}) collective-permute-start(f32[4,42,8,128]{3,2,1,0:T(8,128)S(1)} %get-tuple-element.61), channel_id=1, source_target_pairs={{0,4},{1,5},{2,6},{3,7},{4,8},{5,9},{6,10},{7,11},{8,12},{9,13},{1... | collective-permute-start | bytes 2064392 | tf_op jit(solution)/shard_map/ppermute | solution.py:286
  41.8 0.0 collective-permute-done.2.far_o
  41.8 8.6 %collective-permute-start.8 = (f32[6,13,8,128]{3,2,1,0:T(8,128)S(1)}, f32[6,13,8,128]{3,2,1,0:T(8,128)S(1)}, u32[]{:S(2)}, u32[]{:S(2)}) collective-permute-start(f32[6,13,8,128]{3,2,1,0:T(8,128)S(1)} %get-tuple-element.39.after.middle), channel_id=1, source_target_pairs={{0,16},{1,17},{2,18},{3,19},{4,20},{5,21},{6,22},{7,23},{8,24},{9,... | collective-permute-start | bytes 958472 | tf_op jit(solution)/shard_map/ppermute | solution.py:286
  50.4 0.0 collective-permute-done.1.far_p
  50.4 0.0 collective-permute-done.far_m
  50.4 2.5 %square0.1 = (f32[3,208,256]{2,1,0:T(8,128)S(1)}, f32[384,256]{1,0:T(8,128)S(1)}, bf16[1792,256]{1,0:T(8,128)(2,1)S(1)}, bf16[1792,256]{1,0:T(8,128)(2,1)S(1)}, ...) custom-call(s32[12,128]{1,0:T(8,128)S(1)} %get-tuple-element.33.code, ...), custom_call_target="tpu_custom_call" | custom-call | flops 924844032 | bytes 4000000 | tf_op jit(solution)/shard_map/square0/pallas_call | solution.py:329
  52.9 2.2 %collective-permute-start.4 = (f32[384,256]{1,0:T(8,128)S(1)}, f32[384,256]{1,0:T(8,128)S(1)}, u32[]{:S(2)}, u32[]{:S(2)}) collective-permute-start(f32[384,256]{1,0:T(8,128)S(1)} %get-tuple-element.37), channel_id=1, source_target_pairs={{0,496},{1,497},{2,498},{3,499},{4,500},{5,501},{6,502},{7,503},{8... | collective-permute-start | bytes 1179656 | tf_op jit(solution)/shard_map/ppermute | solution.py:286
  55.1 0.7 %third_inner.1 = (f32[3,112,256]{2,1,0:T(8,128)S(1)}, bf16[2,3,208,256]{3,2,1,0:T(8,128)(2,1)S(1)}) custom-call(f32[3,208,256]{2,1,0:T(8,128)S(1)} %get-tuple-element.40.square0, bf16[1792,256]{1,0:T(8,128)(2,1)S(1)} %get-tuple-element.41.rest_0_, bf16[1792,256]{1,0:T(8,128)(2,1)S(1)} %get-tuple-element.42.rest_1_, ...), custom_call_target="tpu_custom_call" | custom-call | flops 396361728 | bytes 4000000 | tf_op jit(solution)/shard_map/third_inner/pallas_call | solution.py:345
  55.8 0.0 collective-permute-done.8.after
  55.8 0.0 collective-permute-done.6.far_p
  55.8 0.0 collective-permute-done.5.far_m
  55.8 2.5 %square1.1 = (f32[3,208,256]{2,1,0:T(8,128)S(1)}, f32[384,256]{1,0:T(8,128)S(1)}, bf16[1792,256]{1,0:T(8,128)(2,1)S(1)}, bf16[1792,256]{1,0:T(8,128)(2,1)S(1)}, ...) custom-call(s32[12,128]{1,0:T(8,128)S(1)} %get-tuple-element.33.code, ...), custom_call_target="tpu_custom_call" | custom-call | flops 924844032 | bytes 4000000 | tf_op jit(solution)/shard_map/square1/pallas_call | solution.py:329
  58.3 7.1 %collective-permute-start.9 = (f32[384,256]{1,0:T(8,128)S(1)}, f32[384,256]{1,0:T(8,128)S(1)}, u32[]{:S(2)}, u32[]{:S(2)}) collective-permute-start(f32[384,256]{1,0:T(8,128)S(1)} %get-tuple-element.49), channel_id=1, source_target_pairs={{0,16},{1,17},{2,18},{3,19},{4,20},{5,21},{6,22},{7,23},{8,24},{9,... | collective-permute-start | bytes 1179656 | tf_op jit(solution)/shard_map/ppermute | solution.py:286
  65.4 1.3 %third_second.1 = (f32[3,112,256]{2,1,0:T(8,128)S(1)}, f32[3,112,256]{2,1,0:T(8,128)S(1)}) custom-call(bf16[2,3,208,256]{3,2,1,0:T(8,128)(2,1)S(1)} %get-tuple-element.51.held0, f32[3,208,256]{2,1,0:T(8,128)S(1)} %get-tuple-element.50.square1, f32[3,112,256]{2,1,0:T(8,128)S(1)} %get-tuple-element.52.before, bf16[1792,256]{1,0:T(8,128)(2,1)S(1)} %get-tuple-element.41.rest_0_, ...), custom_call_target="tpu_custom_call" | custom-call | flops 924844032 | bytes 4000000 | tf_op jit(solution)/shard_map/third_second/pallas_call | solution.py:359
  66.8 0.0 collective-permute-done.4.halo0
  66.8 0.0 collective-permute-done.9.halo1
  66.8 1.9 %finish.1 = f32[12,13,8,128]{3,2,1,0:T(8,128)} custom-call(s32[12,128]{1,0:T(8,128)S(1)} %get-tuple-element.33.codes, f32[384,256]{1,0:T(8,128)S(1)} %collective-permute-done.4.halo0, f32[384,256]{1,0:T(8,128)S(1)} %collective-permute-done.9.halo1, f32[3,208,256]{2,1,0:T(8,128)S(1)} %get-tuple-element.40.square0, ...), custom_call_target="tpu_custom_call" | custom-call | flops 528482304 | bytes 4000000 | tf_op jit(solution)/shard_map/finish/pallas_call | solution.py:369
Async XLA Ops:
  17.8 22.1 %collective-permute-start.7 = (f32[4,42,8,128]{3,2,1,0:T(8,128)S(1)}, f32[4,42,8,128]{3,2,1,0:T(8,128)S(1)}, u32[]{:S(2)}, u32[]{:S(2)}) collective-permute-start(f32[4,42,8,128]{3,2,1,0:T(8,128)S(1)} %get-tuple-element.61), channel_id=1, source_target_pairs={{0,8},{1,9},{2,10},{3,11},{4,12},{5,13},{6,14},{7,15},{8,0},{9,1},... | collective-permute-start | bytes 2064392 | tf_op jit(solution)/shard_map/ppermute | solution.py:286
  22.5 19.3 %collective-permute-start.2 = (f32[4,42,8,128]{3,2,1,0:T(8,128)S(1)}, f32[4,42,8,128]{3,2,1,0:T(8,128)S(1)}, u32[]{:S(2)}, u32[]{:S(2)}) collective-permute-start(f32[4,42,8,128]{3,2,1,0:T(8,128)S(1)} %get-tuple-element.62), channel_id=1, source_target_pairs={{0,8},{1,9},{2,10},{3,11},{4,12},{5,13},{6,14},{7,15},{8,0},{9,1},... | collective-permute-start | bytes 2064392 | tf_op jit(solution)/shard_map/ppermute | solution.py:286
  24.6 11.2 %collective-permute-start.3 = (f32[6,13,8,128]{3,2,1,0:T(8,128)S(1)}, f32[6,13,8,128]{3,2,1,0:T(8,128)S(1)}, u32[]{:S(2)}, u32[]{:S(2)}) collective-permute-start(f32[6,13,8,128]{3,2,1,0:T(8,128)S(1)} %get-tuple-element.35.middle.before), channel_id=1, source_target_pairs={{0,496},{1,497},{2,498},{3,499},{4,500},{5,501},{6,502},{7,503},{8... | collective-permute-start | bytes 958472 | tf_op jit(solution)/shard_map/ppermute | solution.py:286
  30.5 19.8 %collective-permute-start.1 = (f32[4,42,8,128]{3,2,1,0:T(8,128)S(1)}, f32[4,42,8,128]{3,2,1,0:T(8,128)S(1)}, u32[]{:S(2)}, u32[]{:S(2)}) collective-permute-start(f32[4,42,8,128]{3,2,1,0:T(8,128)S(1)} %get-tuple-element.62), channel_id=1, source_target_pairs={{0,12},{1,13},{2,14},{3,15},{4,0},{5,1},{6,2},{7,3},{8,4},{9,5},{1... | collective-permute-start | bytes 2064392 | tf_op jit(solution)/shard_map/ppermute | solution.py:286
  33.3 17.1 %collective-permute-start = (f32[4,42,8,128]{3,2,1,0:T(8,128)S(1)}, f32[4,42,8,128]{3,2,1,0:T(8,128)S(1)}, u32[]{:S(2)}, u32[]{:S(2)}) collective-permute-start(f32[4,42,8,128]{3,2,1,0:T(8,128)S(1)} %get-tuple-element.62), channel_id=1, source_target_pairs={{0,4},{1,5},{2,6},{3,7},{4,8},{5,9},{6,10},{7,11},{8,12},{9,13},{1... | collective-permute-start | bytes 2064392 | tf_op jit(solution)/shard_map/ppermute | solution.py:286
  35.8 20.0 %collective-permute-start.6 = (f32[4,42,8,128]{3,2,1,0:T(8,128)S(1)}, f32[4,42,8,128]{3,2,1,0:T(8,128)S(1)}, u32[]{:S(2)}, u32[]{:S(2)}) collective-permute-start(f32[4,42,8,128]{3,2,1,0:T(8,128)S(1)} %get-tuple-element.61), channel_id=1, source_target_pairs={{0,12},{1,13},{2,14},{3,15},{4,0},{5,1},{6,2},{7,3},{8,4},{9,5},{1... | collective-permute-start | bytes 2064392 | tf_op jit(solution)/shard_map/ppermute | solution.py:286
  39.9 16.0 %collective-permute-start.5 = (f32[4,42,8,128]{3,2,1,0:T(8,128)S(1)}, f32[4,42,8,128]{3,2,1,0:T(8,128)S(1)}, u32[]{:S(2)}, u32[]{:S(2)}) collective-permute-start(f32[4,42,8,128]{3,2,1,0:T(8,128)S(1)} %get-tuple-element.61), channel_id=1, source_target_pairs={{0,4},{1,5},{2,6},{3,7},{4,8},{5,9},{6,10},{7,11},{8,12},{9,13},{1... | collective-permute-start | bytes 2064392 | tf_op jit(solution)/shard_map/ppermute | solution.py:286
  41.8 14.0 %collective-permute-start.8 = (f32[6,13,8,128]{3,2,1,0:T(8,128)S(1)}, f32[6,13,8,128]{3,2,1,0:T(8,128)S(1)}, u32[]{:S(2)}, u32[]{:S(2)}) collective-permute-start(f32[6,13,8,128]{3,2,1,0:T(8,128)S(1)} %get-tuple-element.39.after.middle), channel_id=1, source_target_pairs={{0,16},{1,17},{2,18},{3,19},{4,20},{5,21},{6,22},{7,23},{8,24},{9,... | collective-permute-start | bytes 958472 | tf_op jit(solution)/shard_map/ppermute | solution.py:286
  52.9 13.9 %collective-permute-start.4 = (f32[384,256]{1,0:T(8,128)S(1)}, f32[384,256]{1,0:T(8,128)S(1)}, u32[]{:S(2)}, u32[]{:S(2)}) collective-permute-start(f32[384,256]{1,0:T(8,128)S(1)} %get-tuple-element.37), channel_id=1, source_target_pairs={{0,496},{1,497},{2,498},{3,499},{4,500},{5,501},{6,502},{7,503},{8... | collective-permute-start | bytes 1179656 | tf_op jit(solution)/shard_map/ppermute | solution.py:286
  58.3 8.5 %collective-permute-start.9 = (f32[384,256]{1,0:T(8,128)S(1)}, f32[384,256]{1,0:T(8,128)S(1)}, u32[]{:S(2)}, u32[]{:S(2)}) collective-permute-start(f32[384,256]{1,0:T(8,128)S(1)} %get-tuple-element.49), channel_id=1, source_target_pairs={{0,16},{1,17},{2,18},{3,19},{4,20},{5,21},{6,22},{7,23},{8,24},{9,... | collective-permute-start | bytes 1179656 | tf_op jit(solution)/shard_map/ppermute | solution.py:286
